TPU v7x, 256 devices: a whole 4x4x8 slice. The times are simulated.
256 devices in a mesh: dp: 16 (over y_hi, z), mp: 16 (over y_lo, x, core).
Axes of the slice: x: 4, y: 4 (y_hi: 2, y_lo: 2; y = y_hi * 2 + y_lo), z: 8, core: 2. Of those that a mesh axis runs over, the one named last changes fastest.
Arguments:
- tokens: bfloat16 [64, 257, 1664], P('dp', None, 'mp'), may hold values from -12 to 12
- up_ckpts: bfloat16 [2, 10, 1664, 8192], P(None, None, 'dp', 'mp'), may hold values from -0.3125 to 0.3125
- up_bias_ckpts: float32 [2, 10, 8192], P(None, None, 'mp'), may hold values from -3 to 3
- down_ckpts: bfloat16 [2, 10, 8192, 1664], P(None, None, 'mp', 'dp'), may hold values from -0.125 to 0.125
- down_bias_ckpts: float32 [2, 10, 1664], replicated, may hold values from -1.75 to 1.75
- norm_ckpts: float32 [2, 10, 1664], replicated, may hold values from 0.25 to 1.75
- soup_mask: int32 [10], replicated, may hold values from 0 to 1, as said below
- final_gain: float32 [1664], replicated, may hold values from 0.25 to 1.75
- projection: bfloat16 [1664, 1280], replicated, may hold values from -0.15625 to 0.15625
- class_embed: bfloat16 [22528, 1280], P('dp', 'mp'), may hold values from -0.0625 to 0.0625
- labels: int32 [64], P('dp'), may hold values from 0 to 22527
Outputs:
- logits: float32 [64, 22528], P('dp')
- label_logit: float32 [64], P('dp')
Inputs may be any that keep to these rules, and one draw needn't show every extreme that they name: `soup_mask`: every entry is 0 or 1, and at least one checkpoint is in the soup.
All inputs are finite; a program needn't handle non-finite values.
Results may differ from a plain program's by a relative error of at most 0.025.
Values may be sent and summed in bfloat16 or wider, within the bound.
A program may use at most 128 MiB of HBM per device.

v0:
```python
import jax
import jax.numpy as jnp
from jax import lax
from jax.sharding import PartitionSpec as P

LAYERS = 2


def soup_average(ckpts, share):
    total = jnp.zeros(ckpts.shape[1:], jnp.float32)
    for which in range(ckpts.shape[0]):
        total = total + share[which] * ckpts[which].astype(jnp.float32)
    return total


def layer_norm(values, gain):
    center = values - jnp.mean(values, axis=-1, keepdims=True)
    spread = jnp.mean(center * center, axis=-1, keepdims=True)
    return center * lax.rsqrt(spread + 1e-05) * gain


def gather_rows(values):
    return lax.all_gather(values, "mp", axis=1, tiled=True)


def scatter_terms(terms):
    return lax.psum_scatter(
        terms.astype(jnp.bfloat16), "mp", scatter_dimension=1, tiled=True
    ).astype(jnp.float32)


def per_device(
    tokens,
    up_ckpts,
    up_bias_ckpts,
    down_ckpts,
    down_bias_ckpts,
    norm_ckpts,
    soup_mask,
    final_gain,
    projection,
    class_embed,
    labels,
):
    mask_float = soup_mask.astype(jnp.float32)
    share = mask_float / jnp.sum(mask_float)
    images, token_count, feature_cols = tokens.shape
    row_count = images * token_count
    mp_slot = lax.axis_index("mp")
    up_local = [
        soup_average(up_ckpts[index], share).astype(jnp.bfloat16) for index in range(LAYERS)
    ]
    down_local = [
        soup_average(down_ckpts[index], share).astype(jnp.bfloat16) for index in range(LAYERS)
    ]
    down_biases = [soup_average(down_bias_ckpts[index], share) for index in range(LAYERS)]
    up_whole, down_whole = (
        lax.all_gather(jnp.stack(up_local), "dp", axis=1, tiled=True),
        lax.all_gather(jnp.stack(down_local), "dp", axis=2, tiled=True),
    )

    def up_product(layer_index, normed):
        return jnp.dot(normed, up_whole[layer_index], preferred_element_type=jnp.float32)

    def down_terms(layer_index, hidden):
        return jnp.dot(hidden, down_whole[layer_index], preferred_element_type=jnp.float32)

    def mlp_terms(layer_index, full_rows):
        norm_gain = soup_average(norm_ckpts[layer_index], share)
        up_bias = soup_average(up_bias_ckpts[layer_index], share)
        normed = layer_norm(full_rows.astype(jnp.float32), norm_gain).astype(jnp.bfloat16)
        hidden = jax.nn.gelu(up_product(layer_index, normed) + up_bias, approximate=False).astype(
            jnp.bfloat16
        )
        return down_terms(layer_index, hidden)

    def own_columns(values):
        return lax.dynamic_slice_in_dim(
            values, mp_slot * feature_cols, feature_cols, values.ndim - 1
        )

    shard = tokens.reshape(row_count, feature_cols)
    last_layer = LAYERS - 1
    layer_index = 0
    summed = scatter_terms(mlp_terms(layer_index, gather_rows(shard)))
    shard = (shard.astype(jnp.float32) + own_columns(down_biases[layer_index]) + summed).astype(
        jnp.bfloat16
    )
    full_rows = gather_rows(shard)
    summed = scatter_terms(mlp_terms(last_layer, full_rows))
    final = shard.astype(jnp.float32) + own_columns(down_biases[last_layer]) + summed
    pooled = jnp.mean(final.reshape(images, token_count, feature_cols), axis=1).astype(jnp.bfloat16)
    pooled_full = gather_rows(pooled)
    pooled_norm = layer_norm(pooled_full.astype(jnp.float32), final_gain).astype(jnp.bfloat16)
    embedding = jnp.dot(pooled_norm, projection, preferred_element_type=jnp.float32)
    unit_rows = (
        embedding * lax.rsqrt(jnp.sum(embedding * embedding, axis=1, keepdims=True) + 1e-06)
    ).astype(jnp.bfloat16)
    embed_cols = class_embed.shape[1]
    unit_cols = lax.dynamic_slice_in_dim(unit_rows, mp_slot * embed_cols, embed_cols, 1)
    block = lax.dot_general(
        unit_cols,
        lax.all_gather(class_embed, "dp", axis=0, tiled=True),
        (((1,), (1,)), ((), ())),
        preferred_element_type=jnp.float32,
    )
    logits = lax.psum(block, "mp") * 100.0
    matches = lax.broadcasted_iota(jnp.int32, logits.shape, 1) == labels[:, None]
    label_logit = jnp.sum(jnp.where(matches, logits, 0.0), axis=1)
    return (logits, label_logit)


def solution(mesh):
    placed = (
        P("dp", None, "mp"),
        P(None, None, "dp", "mp"),
        P(None, None, "mp"),
        P(None, None, "mp", "dp"),
        P(),
        P(),
        P(),
        P(),
        P(),
        P("dp", "mp"),
        P("dp"),
    )
    return jax.shard_map(
        per_device, mesh=mesh, in_specs=placed, out_specs=(P("dp", None), P("dp")), check_vma=False
    )
```

profile of v0, /device:TPU:1, one launch (start us, length us, event | category | flops | bytes accessed | tf_op | source)
XLA Modules:
  0.0 682.3 jit_solution(10228581780715219898)
XLA Ops:
  7.2 1.1 copy.26
  9.4 1.3 convert_reduce_fusion.3
  10.7 1.3 convert_divide_fusion
  12.6 7.9 %fusion.54 = bf16[1,104,512]{2,1,0:T(8,128)(2,1)S(1)} fusion(bf16[2,10,104,512]{3,2,1,0:T(8,128)(2,1)} %param.12, f32[]{:T(128)} %bitcast.9, f32[]{:T(128)} %bitcast.8, f32[]{:T(128)} %bitcast.7, f32[]{:T(128)} %bitcast.6, f32[]{:T(128)} %bitcast.5, f32[]{:T(128)} %bitcast.4, f32[]{:T(128)} %bitcast.3, f32[]{:T(128)} %bitcast.2, f32[]{:T(128)} %bitcast.1, ...), kind=kLoop, calls=%fused_computation.79 | loop fusion | flops 1597440 | bytes 1171496 | tf_op jit(solution)/shard_map/convert_element_type | solution.py:51
  20.6 6.6 fusion.55
  28.0 7.9 %fusion.56 = bf16[1,512,104]{1,2,0:T(8,128)(2,1)S(1)} fusion(bf16[2,10,512,104]{2,3,1,0:T(8,128)(2,1)} %param.14, f32[]{:T(128)} %bitcast.9, f32[]{:T(128)} %bitcast.8, f32[]{:T(128)} %bitcast.7, f32[]{:T(128)} %bitcast.6, f32[]{:T(128)} %bitcast.5, f32[]{:T(128)} %bitcast.4, f32[]{:T(128)} %bitcast.3, f32[]{:T(128)} %bitcast.2, f32[]{:T(128)} %bitcast.1, ...), kind=kLoop, calls=%fused_computation.81 | loop fusion | flops 1597440 | bytes 1171496 | tf_op jit(solution)/shard_map/convert_element_type | solution.py:54
  35.9 7.9 %fusion.57 = bf16[1,512,104]{1,2,0:T(8,128)(2,1)S(1)} fusion(bf16[2,10,512,104]{2,3,1,0:T(8,128)(2,1)} %param.14, f32[]{:T(128)} %bitcast.9, f32[]{:T(128)} %bitcast.8, f32[]{:T(128)} %bitcast.7, f32[]{:T(128)} %bitcast.6, f32[]{:T(128)} %bitcast.5, f32[]{:T(128)} %bitcast.4, f32[]{:T(128)} %bitcast.3, f32[]{:T(128)} %bitcast.2, f32[]{:T(128)} %bitcast.1, ...), kind=kLoop, calls=%fused_computation.82 | loop fusion | flops 1597440 | bytes 1171496 | tf_op jit(solution)/shard_map/convert_element_type | solution.py:54
  44.6 6.5 add_reduce_fusion.1
  51.1 6.4 add_add_fusion.1
  57.6 2.8 convert_reduce_fusion.1
  61.9 86.1 %all-gather.9.cloned.1.call-done = bf16[2,1664,512]{2,1,0:T(8,128)(2,1)} async-done(((bf16[2,104,512]{2,1,0:T(8,128)(2,1)}), bf16[2,1664,512]{2,1,0:T(8,128)(2,1)}) %all-gather.9.cloned.1.call-update) | async-done | bytes 3407888 | tf_op jit(solution)/shard_map/all_gather | solution.py:58
  148.1 94.2 %all-gather.11.cloned.1.call-done = bf16[2,512,1664]{1,2,0:T(8,128)(2,1)} async-done(((bf16[2,512,104]{1,2,0:T(8,128)(2,1)}), bf16[2,512,1664]{1,2,0:T(8,128)(2,1)}) %all-gather.11.cloned.1.call-update) | async-done | bytes 3407888 | tf_op jit(solution)/shard_map/all_gather | solution.py:59
  242.3 13.8 %convolution_convert_fusion.1 = bf16[1028,1664]{0,1:T(8,128)(2,1)} fusion(bf16[2,512,1664]{1,2,0:T(8,128)(2,1)} %all-gather.11.cloned.1.call-done, bf16[1028,1664]{0,1:T(8,128)(2,1)} %all-gather.7.cloned.1.call-done, f32[1664]{0:T(1024)S(1)} %add_reduce_fusion.1, f32[1028]{0:T(1024)S(1)} %add_rsqrt_fusion.1, f32[1028]{0:T(1024)S(1)} %broadcast_multiply_fusion.2, ...), kind=kOutput, calls=%fused_computation.15 | convolution fusion | flops 3548294144 | bytes 10679840 | tf_op jit(solution)/shard_map/dot_general | solution.py:66
  257.0 2.5 fusion.152
  259.5 3.2 multiply_add_fusion
  262.7 3.3 fusion.91
  266.1 57.2 %reduce-scatter.9.cloned.1.call-done = bf16[1028,104]{0,1:T(8,128)(2,1)} async-done(((bf16[1028,1664]{0,1:T(8,128)(2,1)}), bf16[1028,104]{0,1:T(8,128)(2,1)}) %reduce-scatter.9.cloned.1.call-update) | async-done | bytes 213840
  323.3 1.1 copy.28
  325.6 6.5 add_reduce_fusion
  332.1 6.4 add_add_fusion
  338.6 28.8 %all-gather.13.cloned.1.call-done = bf16[1028,1664]{0,1:T(8,128)(2,1)} async-done(((bf16[1028,104]{0,1:T(8,128)(2,1)}), bf16[1028,1664]{0,1:T(8,128)(2,1)}) %all-gather.13.cloned.1.call-update) | async-done | bytes 3421200 | tf_op jit(solution)/shard_map/all_gather | solution.py:23
  367.4 2.8 convert_reduce_fusion
  371.7 13.7 %convolution_convert_fusion = bf16[1028,1664]{0,1:T(8,128)(2,1)} fusion(bf16[2,512,1664]{1,2,0:T(8,128)(2,1)} %all-gather.11.cloned.1.call-done, bf16[1028,1664]{0,1:T(8,128)(2,1)} %all-gather.13.cloned.1.call-done, f32[1664]{0:T(1024)S(1)} %add_reduce_fusion, f32[1028]{0:T(1024)S(1)} %add_rsqrt_fusion, f32[1028]{0:T(1024)S(1)} %broadcast_multiply_fusion.1, ...), kind=kOutput, calls=%fused_computation.14 | convolution fusion | flops 3548294144 | bytes 10679840 | tf_op jit(solution)/shard_map/dot_general | solution.py:66
  386.2 3.3 fusion.90
  389.6 62.7 %reduce-scatter.11.cloned.1.call-done = bf16[1028,104]{0,1:T(8,128)(2,1)} async-done(((bf16[1028,1664]{0,1:T(8,128)(2,1)}), bf16[1028,104]{0,1:T(8,128)(2,1)}) %reduce-scatter.11.cloned.1.call-update) | async-done | bytes 213840
  452.3 1.1 copy.30
  453.6 20.0 %all-gather = bf16[16,104,4]{1,2,0:T(4,128)(2,1)S(1)} all-gather(bf16[1,104,4]{1,2,0:T(4,128)(2,1)S(1)} %fusion.64), channel_id=1, replica_groups=mesh['dp'=16,'mp'=16] {'mp'}, dimensions={0}, use_global_device_ids=true | all-gather | bytes 14144 | tf_op jit(solution)/shard_map/all_gather | solution.py:23
  474.1 3.0 multiply_reduce_fusion.1
  477.1 72.9 %all-gather.15.cloned.1.call-done = bf16[22528,80]{0,1:T(8,128)(2,1)} async-done(((bf16[1408,80]{0,1:T(8,128)(2,1)}), bf16[22528,80]{0,1:T(8,128)(2,1)}) %all-gather.15.cloned.1.call-update) | async-done | bytes 3604496 | tf_op jit(solution)/shard_map/all_gather | solution.py:103
  550.0 3.4 fusion.65
  553.4 119.5 %all-reduce.4.cloned.1.call-done = f32[4,22528]{1,0:T(4,128)} async-done(((f32[4,22528]{1,0:T(4,128)}), f32[4,22528]{1,0:T(4,128)}) %all-reduce.4.cloned.1.call-update) | async-done | bytes 360464 | tf_op jit(solution)/shard_map/psum | solution.py:107
  673.0 2.5 select_reduce_fusion
  (57 shorter events, 9.8 us)
Async XLA Ops:
  7.2 13.4 %copy-start.2 = (bf16[2,10,104,512]{3,2,1,0:T(8,128)(2,1)S(1)}, bf16[2,10,104,512]{3,2,1,0:T(8,128)(2,1)}, u32[]{:S(2)}) copy-start(bf16[2,10,104,512]{3,2,1,0:T(8,128)(2,1)} %param.12) | copy-start | bytes 6389764
  7.2 50.4 %all-gather.7.cloned.1.call-start = ((), (), s32[]{:S(2)}) async-start(), calls=%async_computation.2 | async-start | bytes 4073472 | tf_op jit(solution)/shard_map/all_gather | solution.py:23
  9.3 138.7 %all-gather.9.cloned.1.call-start = ((), (), s32[]{:S(2)}) async-start(), calls=%async_computation.3 | async-start | bytes 3620864 | tf_op jit(solution)/shard_map/all_gather | solution.py:58
  27.2 17.4 %copy-start.3 = (f32[2,10,1664]{2,0,1:T(2,128)S(1)}, f32[2,10,1664]{2,0,1:T(2,128)}, u32[]{:S(2)}) copy-start(f32[2,10,1664]{2,0,1:T(2,128)} %param.16) | copy-start | bytes 399364
  27.2 23.9 %copy-start.5 = (f32[2,10,512]{2,0,1:T(2,128)S(1)}, f32[2,10,512]{2,0,1:T(2,128)}, u32[]{:S(2)}) copy-start(f32[2,10,512]{2,0,1:T(2,128)} %param.13) | copy-start | bytes 122884
  27.9 214.4 %all-gather.11.cloned.1.call-start = ((), (), s32[]{:S(2)}) async-start(), calls=%async_computation.4 | async-start | bytes 3620864 | tf_op jit(solution)/shard_map/all_gather | solution.py:59
  44.6 278.7 %reduce-scatter.9.cloned.1.call-start = ((), (), s32[]{:S(2)}) async-start(), calls=%async_computation.8 | async-start | bytes 4073472
  57.6 3.2 copy-start
  256.1 0.9 copy-start.4
  256.1 111.3 %all-gather.13.cloned.1.call-start = ((), (), s32[]{:S(2)}) async-start(), calls=%async_computation.5 | async-start | bytes 4073472 | tf_op jit(solution)/shard_map/all_gather | solution.py:23
  325.4 126.8 %reduce-scatter.11.cloned.1.call-start = ((), (), s32[]{:S(2)}) async-start(), calls=%async_computation.9 | async-start | bytes 4073472
  367.4 3.2 copy-start.1
  385.4 88.6 %copy-start.6 = (f32[1664]{0:T(1024)S(1)}, f32[1664]{0:T(1024)}, u32[]{:S(2)}) copy-start(f32[1664]{0:T(1024)} %param.18) | copy-start | bytes 19972
  385.4 164.5 %all-gather.15.cloned.1.call-start = ((), (), s32[]{:S(2)}) async-start(), calls=%async_computation.6 | async-start | bytes 3829760 | tf_op jit(solution)/shard_map/all_gather | solution.py:103
  386.2 286.8 %all-reduce.4.cloned.1.call-start = ((), (), s32[]{:S(2)}) async-start(), calls=%async_computation.7 | async-start | bytes 720896 | tf_op jit(solution)/shard_map/psum | solution.py:107
  550.0 123.0 %copy-start.7 = (s32[4]{0:T(128)S(1)}, s32[4]{0:T(128)}, u32[]{:S(2)}) copy-start(s32[4]{0:T(128)} %param.21) | copy-start | bytes 52
Sparse Core Ops, SparseCore 0:
  10.5 43.4 all-gather.6
  56.6 91.4 all-gather.8
  150.7 91.5 all-gather.10
  256.2 67.0 reduce-scatter.8
  325.6 41.7 all-gather.12
  385.5 66.6 reduce-scatter.10
  454.9 95.0 all-gather.14
  553.5 119.3 all-reduce.3
where the time goes:
time: 686 us; the launch traced here: 682 us
  waiting for transfers between devices  522 us (76%)
  other arithmetic  83.6 us (12%)
  matrix products  33.9 us (5%)
  blocking collectives  20 us (3%)
  between operations  14.3 us (2%)
  local copies, waits for them, and re-layouts  7.64 us (1%)
    unnamed x10, waiting for transfers between devices  121 us
    psum x1, waiting for transfers between devices, per_device(): logits = lax.psum(block, 'mp') * 100.0  120 us
    all_gather x1, waiting for transfers between devices, per_device(): lax.all_gather(jnp.stack(down_local), 'dp', axis=2, tiled=True)  94.2 us
    all_gather x1, waiting for transfers between devices, per_device(): lax.all_gather(jnp.stack(up_local), 'dp', axis=1, tiled=True)  86.1 us
    all_gather x1, waiting for transfers between devices, per_device(): lax.all_gather(class_embed, 'dp', axis=0, tiled=True)  72.9 us
    add x5, other arithmetic, soup_average(): total = total + share[which] * ckpts[which].astype(jnp.float32)  29.1 us
    all_gather x2, waiting for transfers between devices, gather_rows(): return lax.all_gather(values, 'mp', axis=1, tiled=True)  28.8 us
    dot_general x2, matrix products, down_terms(): jnp.dot(hidden, down_whole[layer_index], preferred_element_type=jnp.float32)  27.5 us
  transfers between devices with their start and end apart: 8, of which 7 were waited for; matrix products, arithmetic and copies ran while one was open for 12% of the time, Pallas kernels for 0%

commit v1 on v0

v1 whole, which is shorter than its diff:
```python
import functools

import jax
import jax.numpy as jnp
from jax import lax
from jax.experimental import pallas as pl
from jax.experimental.pallas import tpu as pltpu
from jax.sharding import PartitionSpec as P

MESH = pl.DeviceIdType.MESH
F32 = jnp.float32
BF16 = jnp.bfloat16

CKPT = 10
D = 1664
DB = 104
FFB = 512
EMB = 1280
EMBB = 80
TOKS = 257
ROWS = 1040
OWN = 80
CHUNK = 208
HALF = 528
CLS_BLOCKS = 11
UP1, DOWN1, UP2, DOWN2 = 0, 1, 2, 3


def layer_norm(values, gain):
    center = values - jnp.mean(values, axis=-1, keepdims=True)
    spread = jnp.mean(center * center, axis=-1, keepdims=True)
    return center * lax.rsqrt(spread + 1e-05) * gain


def gelu(values):
    return 0.5 * values * (1.0 + lax.erf(values * 0.7071067811865476))


def kernel(
    mask, tok, up_ck, down_ck, up_b, down_b, norm_g, final_gain, proj_hbm, cet, labels,
    out, lab_out,
    a2a, state, x1, x2, gath, w_up1, w_dn1, w_up2, w_dn2, hid, p_sib, s_sib, t_own, red,
    tsp, part, part_r, pooled_all, bias2, proj, unit_b, unit_g, unit_f, cls, lg, lgf, lr, ob,
    s_a2a, r_a2a, s_ag, r_ag, s_sb, r_sb, s_ring, r_ring, s_rs, r_rs, s_half, r_half,
    s_pr, r_pr, s_pf, r_pf, s_cl, r_cl, s_un, r_un, s_lg, r_lg, s_ob, r_ob, s_ob2, r_ob2, proj_sem,
):
    dp = lax.axis_index("dp")
    mp = lax.axis_index("mp")
    yh, z = lax.div(dp, 8), lax.rem(dp, 8)
    core = lax.rem(mp, 2)
    chip = lax.div(mp, 2)
    other_yh = 1 - yh
    block = core * 8 + chip
    last = block == 15
    sibling = chip * 2 + (1 - core)

    def copy(src, dst, ssem, rsem, to_dp, to_mp):
        return pltpu.make_async_remote_copy(
            src_ref=src, dst_ref=dst, send_sem=ssem, recv_sem=rsem,
            device_id={"dp": to_dp, "mp": to_mp}, device_id_type=MESH,
        )

    def got(ref, rsem):
        copy(ref, ref, s_half.at[0], rsem, dp, sibling).wait_recv()

    def sent(ref, ssem):
        copy(ref, ref, ssem, r_half.at[0], dp, sibling).wait_send()

    def loop(lo, hi, body):
        def step(k, carry):
            body(k)
            return carry

        lax.fori_loop(lo, hi, step, 0)

    red[:, 64:80, :] = jnp.zeros((8, 16, D), BF16)
    barrier = pltpu.get_barrier_semaphore()

    def greet(k):
        pl.semaphore_signal(
            barrier, inc=1, device_id={"dp": dp, "mp": lax.rem(mp + k, 16)}, device_id_type=MESH
        )
        pl.semaphore_signal(
            barrier, inc=1, device_id={"dp": lax.rem(dp + k, 16), "mp": mp}, device_id_type=MESH
        )

    loop(1, 16, greet)

    proj_copy = pltpu.make_async_copy(proj_hbm, proj, proj_sem)
    proj_copy.start()

    mask_f = [mask[i].astype(F32) for i in range(CKPT)]
    total = mask_f[0]
    for i in range(1, CKPT):
        total = total + mask_f[i]
    total_v = jnp.full((1, 128), total, F32)
    share_v = [jnp.full((1, 128), v, F32) / total_v for v in mask_f]

    def soup_vec(ref, layer, width):
        acc = jnp.zeros((1, width), F32)
        for i in range(CKPT):
            acc = acc + jnp.tile(share_v[i], (1, width // 128)) * ref[layer, i : i + 1, :]
        return acc

    def soup_up(layer, cs):
        acc = jnp.zeros((DB, 128), F32)
        for i in range(CKPT):
            acc = acc + share_v[i] * up_ck[layer, i, :, 128 * cs : 128 * cs + 128].astype(F32)
        return acc

    def soup_down(layer, cs):
        acc = jnp.zeros((128, DB), F32)
        for i in range(CKPT):
            acc = acc + share_v[i][:, :DB] * down_ck[layer, i, 128 * cs : 128 * cs + 128, :].astype(F32)
        tsp[:, :DB] = acc
        return tsp[...].T[:DB]

    def own_shard(t, soup, layer):
        for h in range(2):
            both = jnp.concatenate([soup(layer, h), soup(layer, 2 + h)], axis=0)
            gath[t, dp, :, 128 * h : 128 * h + 128] = both.astype(BF16)

    z_next, z_prev = yh * 8 + lax.rem(z + 1, 8), yh * 8 + lax.rem(z + 7, 8)

    def slot(which_yh, shift):
        return which_yh * 8 + lax.rem(z + shift + 8, 8)

    def ring_push(t, s, n, to):
        copy(gath.at[t, s], gath.at[t, s], s_ring.at[t, n], r_ring.at[t, n], to, mp).start()

    def ring_got(t, s, n):
        got(gath.at[t, s], r_ring.at[t, n])

    def ring(t, step):
        if step == 0:
            ring_push(t, dp, 14, other_yh * 8 + z)
            ring_push(t, dp, 0, z_next)
            ring_push(t, dp, 7, z_prev)
        elif step == 1:
            s = slot(other_yh, 0)
            ring_got(t, s, 14)
            ring_push(t, s, 1, z_next)
            ring_push(t, s, 8, z_prev)
        elif step < 8:
            n = step - 2
            dist = n // 2 + 1
            which = yh if n % 2 == 0 else other_yh
            sl, sr = slot(which, -dist), slot(which, dist)
            ring_got(t, sl, n)
            if n < 5:
                ring_push(t, sl, n + 2, z_next)
            ring_got(t, sr, 7 + n)
            if n < 4:
                ring_push(t, sr, 7 + n + 2, z_prev)
            elif n == 5:
                ring_push(t, sr, 7 + 6, z_prev)
        else:
            ring_got(t, slot(yh, 4), 6)
            ring_got(t, slot(other_yh, 4), 13)

    def compact(t, dst):
        def pair(j):
            g0 = gath[t, 2 * j].astype(F32)
            g1 = gath[t, 2 * j + 1].astype(F32)
            rows = pl.ds(pl.multiple_of(208 * j, 16), 208)
            dst[rows, 0:256] = jnp.concatenate([g0[:DB], g1[:DB]], axis=0).astype(BF16)
            dst[rows, 256:512] = jnp.concatenate([g0[DB:], g1[DB:]], axis=0).astype(BF16)

        loop(0, 8, pair)

    def owner_rows(c, p):
        return pl.multiple_of(512 * c + 64 * p, 16)

    def to_chip(k):
        return lax.rem(chip + k, 8)

    def from_chip(k):
        return lax.rem(chip + 8 - k, 8)

    def ag_start(lay, x):
        mine = x.at[pl.ds(owner_rows(core, chip), 64)]

        def push(k):
            copy(mine, mine, s_ag.at[lay, k], r_ag.at[lay, k], dp, to_chip(k) * 2 + core).start()

        loop(1, 8, push)
        copy(mine, mine, s_sb.at[lay, 0], r_sb.at[lay, 0], dp, sibling).start()
        extra = x.at[pl.ds(1024, 16)]

        @pl.when(last)
        def _():
            def push_extra(k):
                copy(
                    extra, extra, s_ag.at[lay, 8 + k], r_ag.at[lay, 8], dp, to_chip(k) * 2 + core
                ).start()

            loop(1, 8, push_extra)
            copy(extra, extra, s_sb.at[lay, 8], r_sb.at[lay, 8], dp, sibling).start()

    def ag_step(lay, x, k):
        rows = x.at[pl.ds(owner_rows(core, from_chip(k)), 64)]
        got(rows, r_ag.at[lay, k])
        copy(rows, rows, s_sb.at[lay, k], r_sb.at[lay, k], dp, sibling).start()

    def ag_extra(lay, x):
        extra = x.at[pl.ds(1024, 16)]

        @pl.when(jnp.logical_and(core == 1, chip != 7))
        def _():
            got(extra, r_ag.at[lay, 8])
            copy(extra, extra, s_sb.at[lay, 8], r_sb.at[lay, 8], dp, sibling).start()

    def ag_finish(lay, x):
        def step(k):
            got(x.at[pl.ds(owner_rows(1 - core, from_chip(k)), 64)], r_sb.at[lay, k])

        loop(0, 8, step)

        @pl.when(core == 0)
        def _():
            got(x.at[pl.ds(1024, 16)], r_sb.at[lay, 8])

    def ag_sent(lay, x):
        rows = x.at[pl.ds(0, 64)]
        extra = x.at[pl.ds(1024, 16)]

        def step(k):
            sent(rows, s_ag.at[lay, k])

        loop(1, 8, step)

        def step_sb(k):
            sent(rows, s_sb.at[lay, k])

        loop(0, 8, step_sb)

        @pl.when(last)
        def _():
            def step_extra(k):
                sent(extra, s_ag.at[lay, 8 + k])

            loop(1, 8, step_extra)

        @pl.when(core == 1)
        def _():
            sent(extra, s_sb.at[lay, 8])

    def normed_rows(x, gain):
        rows = layer_norm(state[...], gain).astype(BF16)
        x[pl.ds(owner_rows(core, chip), 64), :] = rows[:64]

        @pl.when(last)
        def _():
            x[1024:1040, :] = rows[64:]

    def up_chunk(x, w, bias, ch):
        rows = pl.ds(CHUNK * ch, CHUNK)
        return gelu(jnp.dot(x[rows, :], w[...], preferred_element_type=F32) + bias).astype(BF16)

    def down_chunk(first):
        return lax.dot_general(
            hid[pl.ds(pl.multiple_of(first, 16), 176), :], w_dn1[...],
            (((1,), (1,)), ((), ())), preferred_element_type=F32,
        )

    own_shard(UP1, soup_up, 0)
    pl.semaphore_wait(barrier, 30)

    def send_tokens(k):
        m2 = lax.rem(mp + k, 16)
        src = tok.at[pl.ds(owner_rows(lax.rem(m2, 2), lax.div(m2, 2)), OWN)]
        copy(src, a2a.at[mp], s_a2a.at[k], r_a2a.at[k], dp, m2).start()

    loop(1, 16, send_tokens)
    ring(UP1, 0)
    a2a[mp] = tok[pl.ds(owner_rows(core, chip), OWN), :]
    own_shard(DOWN1, soup_down, 0)
    ring(UP1, 1)
    ring(DOWN1, 0)
    gain1 = soup_vec(norm_g, 0, D)
    ring(UP1, 2)

    def wait_tokens(k):
        got(a2a.at[lax.rem(mp + 16 - k, 16)], r_a2a.at[k])

    loop(1, 16, wait_tokens)
    for j in range(16):
        state[:, DB * j : DB * j + DB] = a2a[j, :, :DB].astype(F32)
    normed_rows(x1, gain1)
    ag_start(0, x1)
    ring(UP1, 3)
    own_shard(UP2, soup_up, 1)
    ring(UP1, 4)
    own_shard(DOWN2, soup_down, 1)
    ring(UP1, 5)
    ring(DOWN1, 1)
    ring(UP1, 6)
    def send_cls(k):
        @pl.when(k != mp)
        def _():
            src = cet.at[:, pl.ds(pl.multiple_of(128 * k, 128), 128)]
            copy(src, cls.at[mp], s_cl.at[k], r_cl.at[mp], dp, k).start()

        @pl.when(k == mp)
        def _():
            cls[mp] = cet[:, pl.ds(pl.multiple_of(128 * k, 128), 128)]

    ag_step(0, x1, 1)
    ag_step(0, x1, 7)
    ring(UP1, 7)
    ring(DOWN1, 2)
    ag_step(0, x1, 2)
    ag_step(0, x1, 6)
    ring(UP1, 8)
    compact(UP1, w_up1)
    ring(DOWN1, 3)
    ag_step(0, x1, 3)
    ag_step(0, x1, 5)
    ring(DOWN1, 4)
    ag_step(0, x1, 4)
    ag_extra(0, x1)
    ring(DOWN1, 5)
    bias_up1 = soup_vec(up_b, 0, FFB)
    ag_finish(0, x1)
    for ch in range(5):
        hid[CHUNK * ch : CHUNK * ch + CHUNK, :] = up_chunk(x1, w_up1, bias_up1, ch)
        if ch == 1:
            ring(DOWN1, 6)
        if ch == 3:
            ring(DOWN1, 7)
    ring(UP2, 0)
    ring(DOWN1, 8)
    compact(DOWN1, w_dn1)
    ring(UP2, 1)

    for i in range(3):
        rows = pl.ds(176 * i, 176)
        p_sib[rows, :] = down_chunk(512 * (1 - core) + 176 * i).astype(BF16)
        copy(
            p_sib.at[rows], s_sib.at[rows], s_half.at[i], r_half.at[i], dp, sibling
        ).start()
    ring(UP2, 2)
    done = 0
    for i in range(3):
        rows = pl.ds(176 * i, 176)
        term = down_chunk(512 * core + 176 * i)
        got(s_sib.at[rows], r_half.at[i])
        t_own[rows, :] = (term + s_sib[rows, :].astype(F32)).astype(BF16)
        upto = min((176 * (i + 1)) // 64, 8)
        for q in range(done, upto):
            @pl.when(chip != q)
            def _(q=q):
                copy(
                    t_own.at[pl.ds(64 * q, 64)], red.at[chip, pl.ds(0, 64)],
                    s_rs.at[q], r_rs.at[chip], dp, q * 2 + core,
                ).start()
        done = upto

    @pl.when(jnp.logical_and(core == 1, chip != 7))
    def _():
        copy(
            t_own.at[pl.ds(512, 16)], red.at[chip, pl.ds(64, 16)],
            s_rs.at[8], r_rs.at[8 + chip], dp, 15,
        ).start()

    red[chip] = t_own[pl.ds(pl.multiple_of(64 * chip, 16), OWN), :]
    ring(UP2, 3)
    loop(0, CLS_BLOCKS, send_cls)
    gain2 = soup_vec(norm_g, 1, D)
    bias_down1 = soup_vec(down_b, 0, D)
    bias_up2 = soup_vec(up_b, 1, FFB)
    bias_down2 = soup_vec(down_b, 1, D)
    for k in range(13):
        bias2[k] = jnp.broadcast_to(bias_down2[:, 128 * k : 128 * k + 128], (8, 128))
    ring(UP2, 4)
    ring(UP2, 5)
    ring(UP2, 6)
    for q in range(8):
        @pl.when(chip != q)
        def _(q=q):
            got(red.at[q, pl.ds(0, 64)], r_rs.at[q])

        if q < 7:
            @pl.when(last)
            def _(q=q):
                got(red.at[q, pl.ds(64, 16)], r_rs.at[8 + q])

    summed = red[0].astype(F32)
    for q in range(1, 8):
        summed = summed + red[q].astype(F32)
    state[...] = (state[...] + bias_down1 + summed).astype(BF16).astype(F32)
    normed_rows(x2, gain2)
    ag_start(1, x2)
    ring(UP2, 7)

    row = lax.broadcasted_iota(jnp.int32, (16, OWN), 1)
    img = lax.broadcasted_iota(jnp.int32, (16, OWN), 0)
    real = owner_rows(core, chip) + row
    inside = (real >= TOKS * img) & (real < TOKS * (img + 1)) & (img < 4)
    inside = inside & ((row < 64) | jnp.broadcast_to(last, (16, OWN)))
    state_sum = jnp.dot(
        jnp.where(inside, 1.0, 0.0).astype(BF16), state[...].astype(BF16), preferred_element_type=F32
    )[:8]
    ring(UP2, 8)
    ring(DOWN2, 0)
    compact(UP2, w_up2)
    ring(DOWN2, 1)
    ring(DOWN2, 2)
    ag_step(1, x2, 1)
    ag_step(1, x2, 7)
    ring(DOWN2, 3)
    ag_step(1, x2, 2)
    ag_step(1, x2, 6)
    ring(DOWN2, 4)
    ag_step(1, x2, 3)
    ag_step(1, x2, 5)
    ring(DOWN2, 5)
    ag_step(1, x2, 4)
    ag_extra(1, x2)
    ring(DOWN2, 6)
    ag_finish(1, x2)
    hsum = jnp.zeros((16, FFB), F32)
    for ch in range(5):
        h = up_chunk(x2, w_up2, bias_up2, ch)
        row = lax.broadcasted_iota(jnp.int32, (16, CHUNK), 1) + CHUNK * ch
        img = lax.broadcasted_iota(jnp.int32, (16, CHUNK), 0)
        inside = (row >= TOKS * img) & (row < TOKS * (img + 1)) & (img < 4)
        hsum = hsum + jnp.dot(
            jnp.where(inside, 1.0, 0.0).astype(BF16), h, preferred_element_type=F32
        )
        if ch == 1:
            ring(DOWN2, 7)
    ring(DOWN2, 8)
    compact(DOWN2, w_dn2)

    hmean = hsum[:8] * (1.0 / TOKS)
    high = hmean.astype(BF16)
    low = (hmean - high.astype(F32)).astype(BF16)
    both = lax.dot_general(
        jnp.concatenate([high.astype(F32), low.astype(F32)], axis=0).astype(BF16), w_dn2[...],
        (((1,), (1,)), ((), ())), preferred_element_type=F32,
    )
    partial = both[:8] + both[8:] + state_sum * (1.0 / TOKS)
    for k in range(13):
        part[k] = partial[:, 128 * k : 128 * k + 128]

    def send_part(k):
        @pl.when(k != mp)
        def _():
            copy(part.at[k], part_r.at[mp], s_pr.at[k], r_pr.at[mp], dp, k).start()

        @pl.when(k == mp)
        def _():
            part_r[mp] = part[k]

    loop(0, 13, send_part)

    @pl.when(mp < 13)
    def _():
        def wait_part(k):
            @pl.when(k != mp)
            def _():
                got(part_r.at[k], r_pr.at[k])

        loop(0, 16, wait_part)
        pooled = part_r[0]
        for k in range(1, 16):
            pooled = pooled + part_r[k]
        pooled_all[mp] = (pooled + bias2[mp]).astype(BF16).astype(F32)

        def send_pooled(k):
            copy(
                pooled_all.at[mp], pooled_all.at[mp], s_pf.at[k], r_pf.at[mp], dp,
                lax.rem(mp + k, 16),
            ).start()

        loop(1, 16, send_pooled)

    def wait_pooled(k):
        @pl.when(k != mp)
        def _():
            got(pooled_all.at[k], r_pf.at[k])

    proj_copy.wait()
    loop(0, 13, wait_pooled)
    pooled = jnp.concatenate([pooled_all[k] for k in range(13)], axis=1)
    pooled_norm = layer_norm(pooled, final_gain[...])
    pooled_norm = jnp.concatenate([pooled_norm, jnp.zeros_like(pooled_norm)], axis=0).astype(BF16)
    embedding = jnp.dot(pooled_norm, proj[...], preferred_element_type=F32)[:8]
    unit = embedding * lax.rsqrt(jnp.sum(embedding * embedding, axis=1, keepdims=True) + 1e-06)
    unit_b[40:48, :] = jnp.zeros((8, 128), F32)
    for j in range(10):
        unit_b[4 * j : 4 * j + 4, :] = unit[:4, 128 * j : 128 * j + 128]
    unit_g[dp] = unit_b[...].astype(BF16)

    def send_unit(k):
        copy(
            unit_g.at[dp], unit_g.at[dp], s_un.at[k], r_un.at[k], lax.rem(dp + k, 16), mp
        ).start()

    loop(1, 16, send_unit)

    def wait_cls(k):
        @pl.when(k != mp)
        def _():
            got(cls.at[k], r_cl.at[k])

    @pl.when(mp < CLS_BLOCKS)
    def _():
        loop(0, 16, wait_cls)

    def wait_unit(k):
        got(unit_g.at[lax.rem(dp + 16 - k, 16)], r_un.at[k])

    loop(1, 16, wait_unit)

    @pl.when(mp < CLS_BLOCKS)
    def _():
        for k in range(16):
            unit_f[48 * k : 48 * k + 48, :] = unit_g[k].astype(F32)
        columns = []
        for j in range(10):
            columns.append(
                jnp.concatenate(
                    [unit_f[pl.ds(4 * j + i, 16, stride=48), :] for i in range(4)], axis=0
                )
            )
        lhs = jnp.concatenate(columns, axis=1).astype(BF16)
        rhs = jnp.concatenate([cls[k] for k in range(16)], axis=0)
        lgf[...] = jnp.dot(lhs, rhs, preferred_element_type=F32) * 100.0
        for k in range(16):
            lg[k] = lgf[pl.ds(k, 4, stride=16), :]
        lr[dp] = lg[dp]

        def send_logits(k):
            to = lax.rem(dp + k, 16)
            copy(lg.at[to], lr.at[dp], s_lg.at[k], r_lg.at[k], to, mp).start()

        loop(1, 16, send_logits)

        def wait_logits(k):
            got(lr.at[lax.rem(dp + 16 - k, 16)], r_lg.at[k])

        loop(1, 16, wait_logits)
        for k in range(16):
            lgf[4 * k : 4 * k + 4, :] = lr[k]
        ob[mp] = lgf[...].astype(BF16)

        def send_ob(k):
            copy(
                ob.at[mp], ob.at[mp], s_ob.at[k], r_ob.at[mp], dp, to_chip(k) * 2 + core
            ).start()

        loop(1, 8, send_ob)
        copy(ob.at[mp], ob.at[mp], s_ob2.at[mp], r_ob2.at[mp], dp, sibling).start()

    for k in range(CLS_BLOCKS):
        @pl.when(jnp.logical_and(core == k % 2, mp != k))
        def _(k=k):
            got(ob.at[k], r_ob.at[k])
            copy(ob.at[k], ob.at[k], s_ob2.at[k], r_ob2.at[k], dp, sibling).start()

    for k in range(CLS_BLOCKS):
        @pl.when(core != k % 2)
        def _(k=k):
            got(ob.at[k], r_ob2.at[k])

    found = jnp.zeros((4, 128), F32)
    lane = lax.broadcasted_iota(jnp.int32, (4, 128), 1)
    label = labels[...]
    for k in range(CLS_BLOCKS):
        vals = ob[k].astype(F32)
        for g in range(16):
            first = (g * CLS_BLOCKS + k) * 128
            piece = vals[4 * g : 4 * g + 4]
            out[:, first : first + 128] = piece
            found = found + jnp.where(lane + first == label, piece, 0.0)
    lab_out[...] = jnp.broadcast_to(jnp.sum(found, axis=1, keepdims=True), (4, 128))

    def sent_a2a(k):
        sent(tok.at[pl.ds(0, OWN)], s_a2a.at[k])
        sent(unit_g.at[0], s_un.at[k])

    loop(1, 16, sent_a2a)

    def sent_ring(t):
        def step(n):
            sent(gath.at[t, 0], s_ring.at[t, n])

        loop(0, 15, step)

    loop(0, 4, sent_ring)
    ag_sent(0, x1)
    ag_sent(1, x2)
    for i in range(3):
        sent(p_sib.at[pl.ds(0, 176)], s_half.at[i])

    for q in range(8):
        @pl.when(chip != q)
        def _(q=q):
            sent(t_own.at[pl.ds(0, 64)], s_rs.at[q])

    @pl.when(jnp.logical_and(core == 1, chip != 7))
    def _():
        sent(t_own.at[pl.ds(0, 16)], s_rs.at[8])

    def sent_cls(k):
        @pl.when(k != mp)
        def _():
            sent(cls.at[0], s_cl.at[k])

    loop(0, CLS_BLOCKS, sent_cls)

    def sent_part(k):
        @pl.when(k != mp)
        def _():
            sent(part.at[0], s_pr.at[k])

    loop(0, 13, sent_part)

    @pl.when(mp < 13)
    def _():
        loop(1, 16, lambda k: sent(part.at[0], s_pf.at[k]))

    @pl.when(mp < CLS_BLOCKS)
    def _():
        loop(1, 16, lambda k: sent(lg.at[0], s_lg.at[k]))
        loop(1, 8, lambda k: sent(ob.at[0], s_ob.at[k]))

    for k in range(CLS_BLOCKS):
        @pl.when(core == k % 2)
        def _(k=k):
            sent(ob.at[0], s_ob2.at[k])


def per_device(
    tokens, up_ckpts, up_bias_ckpts, down_ckpts, down_bias_ckpts, norm_ckpts, soup_mask,
    final_gain, projection, class_embed, labels,
):
    images, token_count, feature_cols = tokens.shape
    rows = images * token_count
    tok = jnp.pad(tokens.reshape(rows, feature_cols), ((0, ROWS - rows), (0, 128 - feature_cols)))
    vm = pl.BlockSpec(memory_space=pltpu.VMEM)
    dma = pltpu.SemaphoreType.DMA
    logits, label_logit = pl.pallas_call(
        kernel,
        out_shape=(
            jax.ShapeDtypeStruct((4, 16 * CLS_BLOCKS * 128), F32),
            jax.ShapeDtypeStruct((4, 128), F32),
        ),
        in_specs=[pl.BlockSpec(memory_space=pltpu.SMEM)]
        + [vm] * 7
        + [pl.BlockSpec(memory_space=pl.ANY)]
        + [vm] * 2,
        out_specs=(vm, vm),
        scratch_shapes=[
            pltpu.VMEM((16, OWN, 128), BF16),
            pltpu.VMEM((OWN, D), F32),
            pltpu.VMEM((ROWS, D), BF16),
            pltpu.VMEM((ROWS, D), BF16),
            pltpu.VMEM((4, 16, 2 * DB, 256), BF16),
            pltpu.VMEM((D, FFB), BF16),
            pltpu.VMEM((D, FFB), BF16),
            pltpu.VMEM((D, FFB), BF16),
            pltpu.VMEM((D, FFB), BF16),
            pltpu.VMEM((ROWS, FFB), BF16),
            pltpu.VMEM((HALF, D), BF16),
            pltpu.VMEM((HALF, D), BF16),
            pltpu.VMEM((HALF, D), BF16),
            pltpu.VMEM((8, OWN, D), BF16),
            pltpu.VMEM((128, 128), F32),
            pltpu.VMEM((13, 8, 128), F32),
            pltpu.VMEM((16, 8, 128), F32),
            pltpu.VMEM((13, 8, 128), F32),
            pltpu.VMEM((13, 8, 128), F32),
            pltpu.VMEM((D, EMB), BF16),
            pltpu.VMEM((48, 128), F32),
            pltpu.VMEM((16, 48, 128), BF16),
            pltpu.VMEM((768, 128), F32),
            pltpu.VMEM((16, EMBB, 128), BF16),
            pltpu.VMEM((16, 4, 128), F32),
            pltpu.VMEM((64, 128), F32),
            pltpu.VMEM((16, 4, 128), F32),
            pltpu.VMEM((CLS_BLOCKS, 64, 128), BF16),
            dma((16,)), dma((16,)),
            dma((2, 16)), dma((2, 16)),
            dma((2, 9)), dma((2, 9)),
            dma((4, 15)), dma((4, 15)),
            dma((9,)), dma((16,)),
            dma((3,)), dma((3,)),
            dma((16,)), dma((16,)),
            dma((16,)), dma((16,)),
            dma((16,)), dma((16,)),
            dma((16,)), dma((16,)),
            dma((16,)), dma((16,)),
            dma((8,)), dma((16,)),
            dma((16,)), dma((16,)),
            dma(()),
        ],
        compiler_params=pltpu.CompilerParams(
            collective_id=0, has_side_effects=True, vmem_limit_bytes=60 * 2**20
        ),
    )(
        soup_mask, tok, up_ckpts, down_ckpts, up_bias_ckpts, down_bias_ckpts, norm_ckpts,
        final_gain[None, :], projection, class_embed.T, labels[:, None],
    )
    return (logits, label_logit[:, 0])


def solution(mesh):
    placed = (
        P("dp", None, "mp"),
        P(None, None, "dp", "mp"),
        P(None, None, "mp"),
        P(None, None, "mp", "dp"),
        P(),
        P(),
        P(),
        P(),
        P(),
        P("dp", "mp"),
        P("dp"),
    )
    return jax.shard_map(
        per_device, mesh=mesh, in_specs=placed, out_specs=(P("dp", None), P("dp")), check_vma=False
    )
```

time: 686 us -> 196 us (0.29)
  waiting for transfers between devices: 522 us -> 0 us
  Pallas kernels: 0 us -> 180 us
  other arithmetic: 83.6 us -> 0 us
  matrix products: 33.9 us -> 0 us
  blocking collectives: 20 us -> 0 us
  between operations: 14.3 us -> 0.66 us
  local copies, waits for them, and re-layouts: 7.64 us -> 14.9 us
    all_gather x5 -> x0, waiting for transfers between devices: 282 us -> none  [the longest x1 94.2 us: per_device(): lax.all_gather(jnp.stack(down_local), 'dp', axis=2, tiled=True)]
    pallas_call x0 -> x1, Pallas kernels: none -> 180 us  [per_device(): pl.pallas_call(kernel, out_shape=(jax.ShapeDtypeStruct((4, 16 * CLS_BLOCK...]
    unnamed x10 -> x0, waiting for transfers between devices: 121 us -> none
    psum x1 -> x0, waiting for transfers between devices: 120 us -> none  [per_device(): logits = lax.psum(block, 'mp') * 100.0]
    dot_general x4 -> x0, matrix products: 33.9 us -> none  [the longest x2 27.5 us: down_terms(): jnp.dot(hidden, down_whole[layer_index], preferred_element_type=jnp.float32)]
    convert_element_type x5 -> x0, other arithmetic: 30.5 us -> none  [the longest x2 15.9 us: per_device(): soup_average(down_ckpts[index], share).astype(jnp.bfloat16)]
    add x6 -> x0, other arithmetic: 29.1 us -> none  [the longest x5 29.1 us: soup_average(): total = total + share[which] * ckpts[which].astype(jnp.float32)]
    all_gather x1 -> x0, blocking collectives: 20 us -> none  [gather_rows(): return lax.all_gather(values, 'mp', axis=1, tiled=True)]
  transfers between devices with their start and end apart: 8 -> 0, of which waited for: 7 -> 0; matrix products, arithmetic and copies ran while one was open for 12% -> 0% of each run, Pallas kernels for 0% -> 0%
where the time goes in v1:
time: 196 us
  Pallas kernels  180 us (92%)
  local copies, waits for them, and re-layouts  14.9 us (8%)
    pallas_call x1, Pallas kernels, per_device(): pl.pallas_call(kernel, out_shape=(jax.ShapeDtypeStruct((4, 16 * CLS_BLOCK...  180 us
    unnamed x8, local copies, waits for them, and re-layouts  9.94 us

profile of v1, /device:TPU:1, one launch (start us, length us, event | category | flops | bytes accessed | tf_op | source)
XLA Modules:
  0.0 195.5 jit_solution(14844080769395133564)
XLA Ops:
  0.6 0.0 copy-start
  0.6 1.5 copy.24.labels
  2.1 1.3 broadcast_in_dim.6.final_gain
  3.4 1.4 copy.21.up_b
  4.8 1.6 copy.22.down_b
  6.4 1.6 copy.23.norm_g
  8.0 1.0 copy.19
  9.0 0.1 reshape.7
  9.1 0.8 pad.4.tok
  9.9 0.0 copy-done
  9.9 2.6 %copy.20.down_ck = bf16[2,10,512,104]{3,2,1,0:T(8,128)(2,1)} copy(bf16[2,10,512,104]{2,3,1,0:T(8,128)(2,1)S(1)} %copy-done) | data formatting | bytes 4259840 | tf_op args[3]
  12.5 180.0 %shard_map.122 = (f32[4,22528]{1,0:T(4,128)}, f32[4,128]{1,0:T(4,128)}) custom-call(s32[10]{0:T(128)} %mask.1, bf16[1040,128]{1,0:T(8,128)(2,1)} %pad.4.tok, bf16[2,10,104,512]{3,2,1,0:T(8,128)(2,1)} %up_ck.1, bf16[2,10,512,104]{3,2,1,0:T(8,128)(2,1)} %copy.20.down_ck, f32[2,10,512]{2,1,0:T(8,128)} %copy.21.up_b, f32[2,10,1664]{2,1,0:T(8,128)} %copy.22.down_b, ...), custom_call_target="tpu_custom_call" | custom-call | tf_op jit(solution)/shard_map/pallas_call | solution.py:645
  192.5 1.3 slice_reduce_fusion
  193.8 1.7 copy.26
Async XLA Ops:
  0.6 9.3 %copy-start = (bf16[2,10,512,104]{2,3,1,0:T(8,128)(2,1)S(1)}, bf16[2,10,512,104]{2,3,1,0:T(8,128)(2,1)}, u32[]{:S(2)}) copy-start(bf16[2,10,512,104]{2,3,1,0:T(8,128)(2,1)} %param.14) | copy-start | bytes 6389764

commit v2 on v1

v2 whole, which is shorter than its diff:
```python
import functools

import jax
import jax.numpy as jnp
from jax import lax
from jax.experimental import pallas as pl
from jax.experimental.pallas import tpu as pltpu
from jax.sharding import PartitionSpec as P

MESH = pl.DeviceIdType.MESH
F32 = jnp.float32
BF16 = jnp.bfloat16

CKPT = 10
D = 1664
DB = 104
FFB = 512
EMB = 1280
EMBB = 80
TOKS = 257
ROWS = 1040
OWN = 80
CHUNK = 208
CLS_BLOCKS = 11
UP1, DOWN1, UP2, DOWN2 = 0, 1, 2, 3
PLACES = ((-1, 0), (1, 0), (0, 1), (-1, 1), (1, 1), (2, 0), (2, 1), (0, 0))
STEPS = (2, -1, 1, 0)


def layer_norm(values, gain):
    center = values - jnp.mean(values, axis=-1, keepdims=True)
    spread = jnp.mean(center * center, axis=-1, keepdims=True)
    return center * lax.rsqrt(spread + 1e-05) * gain


def gelu(values):
    return 0.5 * values * (1.0 + lax.erf(values * 0.7071067811865476))


def kernel(
    mask, tok, up_hbm, down_hbm, up_b, down_b, norm_g, final_gain, proj_hbm, cet,
    ob_out,
    up_ck, down_ck, a2a, state, x1, x2, gath, w_up1, w_dn1, w_up2, w_dn2, hid, p_sib, s_sib, t_own,
    red, extra_s, extra_r, part, part_r, pooled_all, bias2, proj, unit_g, cls, lg, lr, ob,
    s_a2a, r_a2a, s_ag, r_ag, s_sb, r_sb, s_ring, r_ring, s_rs, r_rs, s_half, r_half, s_ex, r_ex,
    s_pr, r_pr, s_pf, r_pf, s_cl, r_cl, s_un, r_un, s_us, r_us, s_lg, r_lg, s_ob, r_ob, s_ob2, r_ob2,
    proj_sem, ck_sem,
):
    dp = lax.axis_index("dp")
    mp = lax.axis_index("mp")
    yh, z = lax.div(dp, 8), lax.rem(dp, 8)
    core = lax.rem(mp, 2)
    chip = lax.div(mp, 2)
    yl, xc = lax.div(mp, 8), lax.rem(chip, 4)
    other_yh = 1 - yh
    block = core * 8 + xc * 2 + yl
    last = block == 15
    extra_src = jnp.logical_and(core == 1, block != 15)
    sibling = chip * 2 + (1 - core)

    def device(y, dx):
        return y * 8 + lax.rem(xc + dx + 4, 4) * 2 + core

    right, left, across = device(yl, 1), device(yl, -1), device(1 - yl, 0)

    def copy(src, dst, ssem, rsem, to_dp, to_mp):
        return pltpu.make_async_remote_copy(
            src_ref=src, dst_ref=dst, send_sem=ssem, recv_sem=rsem,
            device_id={"dp": to_dp, "mp": to_mp}, device_id_type=MESH,
        )

    def got(ref, rsem):
        copy(ref, ref, s_half.at[0], rsem, dp, sibling).wait_recv()

    def sent(ref, ssem):
        copy(ref, ref, ssem, r_half.at[0], dp, sibling).wait_send()

    def loop(lo, hi, body):
        def step(k, carry):
            body(k)
            return carry

        lax.fori_loop(lo, hi, step, 0)

    loads = [
        pltpu.make_async_copy(src.at[layer], dst.at[layer], ck_sem.at[n])
        for n, (src, dst, layer) in enumerate(
            ((up_hbm, up_ck, 0), (down_hbm, down_ck, 0), (up_hbm, up_ck, 1), (down_hbm, down_ck, 1))
        )
    ]
    for load in loads:
        load.start()
    proj_copy = pltpu.make_async_copy(proj_hbm, proj, proj_sem)
    proj_copy.start()

    state[64:80, :] = jnp.zeros((16, D), F32)
    extra_r[...] = jnp.zeros((8, 16, D), BF16)
    barrier = pltpu.get_barrier_semaphore()

    def greet(k):
        pl.semaphore_signal(
            barrier, inc=1, device_id={"dp": dp, "mp": lax.rem(mp + k, 16)}, device_id_type=MESH
        )
        pl.semaphore_signal(
            barrier, inc=1, device_id={"dp": lax.rem(dp + k, 16), "mp": mp}, device_id_type=MESH
        )

    loop(1, 16, greet)

    mask_f = [mask[i].astype(F32) for i in range(CKPT)]
    total = mask_f[0]
    for i in range(1, CKPT):
        total = total + mask_f[i]
    total_v = jnp.full((1, 128), total, F32)
    share_v = [jnp.full((1, 128), v, F32) / total_v for v in mask_f]

    def soup_vec(ref, layer, width):
        acc = jnp.zeros((1, width), F32)
        for i in range(CKPT):
            acc = acc + jnp.tile(share_v[i], (1, width // 128)) * ref[i, layer : layer + 1, :]
        return acc

    def soup(ref, layer, cs):
        acc = jnp.zeros((DB, 128), F32)
        for i in range(CKPT):
            acc = acc + share_v[i] * ref[layer, i, :, 128 * cs : 128 * cs + 128].astype(F32)
        return acc

    def own_shard(t, ref, layer):
        loads[t].wait()
        for h in range(2):
            both = jnp.concatenate([soup(ref, layer, h), soup(ref, layer, 2 + h)], axis=0)
            gath[t, dp, :, 128 * h : 128 * h + 128] = both.astype(BF16)

    z_next, z_prev = yh * 8 + lax.rem(z + 1, 8), yh * 8 + lax.rem(z + 7, 8)

    def slot(which_yh, shift):
        return which_yh * 8 + lax.rem(z + shift + 8, 8)

    def ring_push(t, s, n, to):
        copy(gath.at[t, s], gath.at[t, s], s_ring.at[t, n], r_ring.at[t, n], to, mp).start()

    def ring_got(t, s, n):
        got(gath.at[t, s], r_ring.at[t, n])

    def ring(t, step):
        if step == 0:
            ring_push(t, dp, 14, other_yh * 8 + z)
            ring_push(t, dp, 0, z_next)
            ring_push(t, dp, 7, z_prev)
        elif step == 1:
            s = slot(other_yh, 0)
            ring_got(t, s, 14)
            ring_push(t, s, 1, z_next)
            ring_push(t, s, 8, z_prev)
        elif step < 8:
            n = step - 2
            dist = n // 2 + 1
            which = yh if n % 2 == 0 else other_yh
            sl, sr = slot(which, -dist), slot(which, dist)
            ring_got(t, sl, n)
            if n < 5:
                ring_push(t, sl, n + 2, z_next)
            ring_got(t, sr, 7 + n)
            if n < 4:
                ring_push(t, sr, 7 + n + 2, z_prev)
            elif n == 5:
                ring_push(t, sr, 7 + 6, z_prev)
        else:
            ring_got(t, slot(yh, 4), 6)
            ring_got(t, slot(other_yh, 4), 13)

    def compact(t, dst):
        def pair(j):
            g0 = gath[t, 2 * j].astype(F32)
            g1 = gath[t, 2 * j + 1].astype(F32)
            rows = pl.ds(pl.multiple_of(208 * j, 16), 208)
            dst[rows, 0:256] = jnp.concatenate([g0[:DB], g1[:DB]], axis=0).astype(BF16)
            dst[rows, 256:512] = jnp.concatenate([g0[DB:], g1[DB:]], axis=0).astype(BF16)

        loop(0, 8, pair)

    def block_rows(c, dx, y):
        return pl.multiple_of(512 * c + 128 * lax.rem(xc + dx + 4, 4) + 64 * y, 16)

    def half_rows(x, c, idx, h):
        dx, other = PLACES[idx]
        y = 1 - yl if other else yl
        return x.at[pl.ds(block_rows(c, dx, y) + 32 * h, 32)]

    def ag_push(lay, x, idx_here, idx, h, to):
        rows = half_rows(x, core, idx_here, h)
        n = 2 * idx + h
        copy(rows, rows, s_ag.at[lay, n], r_ag.at[lay, n], dp, to).start()

    def ag_sib(lay, x, idx, h):
        rows = half_rows(x, core, idx, h)
        n = 2 * idx + h
        copy(rows, rows, s_sb.at[lay, n], r_sb.at[lay, n], dp, sibling).start()

    def ag_start(lay, x):
        for h in range(2):
            ag_push(lay, x, 7, 0, h, right)
            ag_push(lay, x, 7, 1, h, left)
            ag_push(lay, x, 7, 2, h, across)
        for h in range(2):
            ag_sib(lay, x, 7, h)
        extra = x.at[pl.ds(1024, 16)]

        @pl.when(last)
        def _():
            def push_extra(k):
                copy(
                    extra, extra, s_ex.at[lay, k], r_ex.at[lay], dp, lax.rem(chip + k, 8) * 2 + core
                ).start()

            loop(1, 8, push_extra)
            copy(extra, extra, s_sb.at[lay, 16], r_sb.at[lay, 16], dp, sibling).start()

    def ag_recv(lay, x, idx, h):
        got(half_rows(x, core, idx, h), r_ag.at[lay, 2 * idx + h])
        if idx == 0:
            ag_push(lay, x, 0, 5, h, right)
            if h == 1:
                ag_push(lay, x, 0, 3, h, across)
        elif idx == 1 and h == 1:
            ag_push(lay, x, 1, 4, h, across)
        elif idx == 2 and h == 0:
            ag_push(lay, x, 2, 3, h, right)
            ag_push(lay, x, 2, 4, h, left)
        elif idx == 4:
            ag_push(lay, x, 4, 6, h, left)
        ag_sib(lay, x, idx, h)

    def ag_extra(lay, x):
        extra = x.at[pl.ds(1024, 16)]

        @pl.when(extra_src)
        def _():
            got(extra, r_ex.at[lay])
            copy(extra, extra, s_sb.at[lay, 16], r_sb.at[lay, 16], dp, sibling).start()

    def ag_finish(lay, x):
        for idx in range(8):
            for h in range(2):
                got(half_rows(x, 1 - core, idx, h), r_sb.at[lay, 2 * idx + h])

        @pl.when(core == 0)
        def _():
            got(x.at[pl.ds(1024, 16)], r_sb.at[lay, 16])

    def ag_sent(lay, x):
        rows = x.at[pl.ds(0, 32)]
        extra = x.at[pl.ds(1024, 16)]
        loop(0, 14, lambda n: sent(rows, s_ag.at[lay, n]))
        loop(0, 16, lambda n: sent(rows, s_sb.at[lay, n]))

        @pl.when(last)
        def _():
            loop(1, 8, lambda k: sent(extra, s_ex.at[lay, k]))

        @pl.when(core == 1)
        def _():
            sent(extra, s_sb.at[lay, 16])

    def normed_rows(x, gain):
        rows = layer_norm(state[...], gain).astype(BF16)
        x[pl.ds(block_rows(core, 0, yl), 64), :] = rows[:64]

        @pl.when(last)
        def _():
            x[1024:1040, :] = rows[64:]

    def up_chunk(x, w, bias, ch):
        rows = pl.ds(CHUNK * ch, CHUNK)
        return gelu(jnp.dot(x[rows, :], w[...], preferred_element_type=F32) + bias).astype(BF16)

    def down_product(rows):
        return lax.dot_general(
            rows, w_dn1[...], (((1,), (1,)), ((), ())), preferred_element_type=F32
        )

    def rs_rows(o, y, h):
        return t_own.at[o, pl.ds(pl.multiple_of(64 * y + 32 * h, 16), 32)]

    def rs_push(o, y, kind, h, to):
        n = 2 * kind + h
        copy(rs_rows(o, y, h), red.at[kind, h], s_rs.at[n], r_rs.at[n], dp, to).start()

    def rs_add(o, y, h, *kinds):
        rows = rs_rows(o, y, h)
        acc = rows[...].astype(F32)
        for kind in kinds:
            got(red.at[kind, h], r_rs.at[2 * kind + h])
            acc = acc + red[kind, h].astype(F32)
        rows[...] = acc.astype(BF16)

    own_shard(UP1, up_ck, 0)
    pl.semaphore_wait(barrier, 30)

    def send_tokens(k):
        m2 = lax.rem(mp + k, 16)
        b2 = lax.rem(m2, 2) * 8 + lax.rem(lax.div(m2, 2), 4) * 2 + lax.div(m2, 8)
        src = tok.at[pl.ds(16 * b2, 17)]
        copy(src, a2a.at[mp], s_a2a.at[k], r_a2a.at[k], dp, m2).start()

    loop(1, 16, send_tokens)
    ring(UP1, 0)
    a2a[mp] = tok[pl.ds(16 * block, 17)]
    own_shard(DOWN1, down_ck, 0)
    ring(DOWN1, 0)
    gain1 = soup_vec(norm_g, 0, D)
    ring(UP1, 1)

    def wait_tokens(k):
        got(a2a.at[lax.rem(mp + 16 - k, 16)], r_a2a.at[k])

    loop(1, 16, wait_tokens)
    for j in range(16):
        state[:68, DB * j : DB * j + DB] = a2a[j].astype(F32).reshape(68, DB)
    normed_rows(x1, gain1)
    ag_start(0, x1)
    ring(UP1, 2)
    own_shard(UP2, up_ck, 1)
    ring(UP1, 3)
    for idx in range(3):
        ag_recv(0, x1, idx, 0)
    ring(UP1, 4)
    for idx in range(3):
        ag_recv(0, x1, idx, 1)
    ring(UP1, 5)
    ag_recv(0, x1, 3, 0)
    ag_recv(0, x1, 4, 0)
    ring(UP1, 6)
    ring(DOWN1, 1)
    ag_recv(0, x1, 3, 1)
    ag_recv(0, x1, 4, 1)
    ag_recv(0, x1, 5, 0)
    ring(UP1, 7)
    ring(DOWN1, 2)
    ag_recv(0, x1, 5, 1)
    ag_recv(0, x1, 6, 0)
    ag_recv(0, x1, 6, 1)
    ag_extra(0, x1)
    own_shard(DOWN2, down_ck, 1)
    ring(UP1, 8)
    ring(DOWN1, 3)
    compact(UP1, w_up1)
    bias_up1 = soup_vec(up_b, 0, FFB)
    ag_finish(0, x1)
    for ch in range(5):
        hid[CHUNK * ch : CHUNK * ch + CHUNK, :] = up_chunk(x1, w_up1, bias_up1, ch)
        if ch == 0:
            ring(DOWN1, 4)
        if ch == 2:
            ring(DOWN1, 5)
        if ch == 4:
            ring(DOWN1, 6)

    def send_cls(k):
        @pl.when(k != mp)
        def _():
            src = cet.at[:, pl.ds(pl.multiple_of(128 * k, 128), 128)]
            copy(src, cls.at[mp], s_cl.at[k], r_cl.at[mp], dp, k).start()

        @pl.when(k == mp)
        def _():
            cls[mp] = cet[:, pl.ds(pl.multiple_of(128 * k, 128), 128)]

    loop(0, CLS_BLOCKS, send_cls)
    gain2 = soup_vec(norm_g, 1, D)
    bias_down1 = soup_vec(down_b, 0, D)
    bias_up2 = soup_vec(up_b, 1, FFB)
    bias_down2 = soup_vec(down_b, 1, D)
    for k in range(13):
        bias2[k] = jnp.broadcast_to(bias_down2[:, 128 * k : 128 * k + 128], (8, 128))
    ring(DOWN1, 7)
    ring(UP2, 0)
    ring(UP2, 1)
    ring(DOWN1, 8)
    compact(DOWN1, w_dn1)

    def own_chunk(o):
        dx = STEPS[o]
        size = 144 if dx == 0 else 128
        rows = pl.ds(0, size)
        for c in (1 - core, core):
            lhs = hid[pl.ds(block_rows(c, dx, 0), 128), :]
            if dx == 0:
                lhs = jnp.concatenate([lhs, hid[1024:1040, :]], axis=0)
            term = down_product(lhs)
            if c is not core:
                p_sib[o, rows, :] = term.astype(BF16)
                copy(
                    p_sib.at[o, rows], s_sib.at[o, rows], s_half.at[o], r_half.at[o], dp, sibling
                ).start()
        got(s_sib.at[o, rows], r_half.at[o])
        t_own[o, rows, :] = (term + s_sib[o, rows, :].astype(F32)).astype(BF16)

    own_chunk(0)
    for h in range(2):
        rs_push(0, yl, 0, h, left)
        rs_push(0, 1 - yl, 1, h, right)
    own_chunk(1)
    for h in range(2):
        rs_push(1, 1 - yl, 2, h, left)
    own_chunk(2)
    for h in range(2):
        rs_add(2, 1 - yl, h, 1)
        rs_push(2, 1 - yl, 3, h, right)
        rs_add(1, yl, h, 0)
        rs_push(1, yl, 4, h, left)
    for h in range(2):
        rs_push(2, yl, 5, h, right)
    ring(UP2, 2)
    own_chunk(3)

    @pl.when(extra_src)
    def _():
        copy(
            t_own.at[3, pl.ds(128, 16)], extra_r.at[chip], s_ex.at[0, 0], r_ex.at[2 + chip], dp, 15
        ).start()

    ring(UP2, 3)
    ring(DOWN2, 0)
    for h in range(2):
        rs_add(3, 1 - yl, h, 3, 2)
        rs_push(3, 1 - yl, 6, h, across)
    ring(UP2, 4)
    ring(UP2, 5)
    ring(DOWN2, 1)
    for h in range(2):
        rs_add(3, yl, h, 4, 5, 6)

    @pl.when(last)
    def _():
        extra = t_own[3, 128:144, :].astype(F32)
        for q in range(7):
            got(extra_r.at[q], r_ex.at[2 + q])
            extra = extra + extra_r[q].astype(F32)
        extra_s[...] = extra

    @pl.when(jnp.logical_not(last))
    def _():
        extra_s[...] = jnp.zeros((16, D), F32)

    summed = jnp.concatenate(
        [t_own[3, pl.ds(pl.multiple_of(64 * yl, 16), 64), :].astype(F32), extra_s[...]], axis=0
    )
    state[...] = (state[...] + bias_down1 + summed).astype(BF16).astype(F32)
    normed_rows(x2, gain2)
    ag_start(1, x2)
    ring(UP2, 6)

    row = lax.broadcasted_iota(jnp.int32, (16, OWN), 1)
    img = lax.broadcasted_iota(jnp.int32, (16, OWN), 0)
    inside = ((row & 3) == img) & (row < jnp.where(last, 68, 64))
    state_sum = jnp.dot(
        jnp.where(inside, 1.0, 0.0).astype(BF16), state[...].astype(BF16), preferred_element_type=F32
    )[:8]
    ring(UP2, 7)
    ring(DOWN2, 2)
    for idx in range(3):
        ag_recv(1, x2, idx, 0)
    ring(UP2, 8)
    for idx in range(3):
        ag_recv(1, x2, idx, 1)
    ring(DOWN2, 3)
    ag_recv(1, x2, 3, 0)
    ag_recv(1, x2, 4, 0)
    ring(DOWN2, 4)
    compact(UP2, w_up2)
    ag_recv(1, x2, 3, 1)
    ag_recv(1, x2, 4, 1)
    ag_recv(1, x2, 5, 0)
    ring(DOWN2, 5)
    ag_recv(1, x2, 5, 1)
    ag_recv(1, x2, 6, 0)
    ag_recv(1, x2, 6, 1)
    ag_extra(1, x2)
    ring(DOWN2, 6)
    ag_finish(1, x2)
    hsum = jnp.zeros((16, FFB), F32)
    for ch in range(5):
        h = up_chunk(x2, w_up2, bias_up2, ch)
        row = lax.broadcasted_iota(jnp.int32, (16, CHUNK), 1) + CHUNK * ch
        img = lax.broadcasted_iota(jnp.int32, (16, CHUNK), 0)
        inside = ((row & 3) == img) & (row < 4 * TOKS)
        hsum = hsum + jnp.dot(
            jnp.where(inside, 1.0, 0.0).astype(BF16), h, preferred_element_type=F32
        )
        if ch == 1:
            ring(DOWN2, 7)
    ring(DOWN2, 8)
    compact(DOWN2, w_dn2)

    hmean = hsum[:8] * (1.0 / TOKS)
    high = hmean.astype(BF16)
    low = (hmean - high.astype(F32)).astype(BF16)
    both = lax.dot_general(
        jnp.concatenate([high.astype(F32), low.astype(F32)], axis=0).astype(BF16), w_dn2[...],
        (((1,), (1,)), ((), ())), preferred_element_type=F32,
    )
    partial = both[:8] + both[8:] + state_sum * (1.0 / TOKS)
    for k in range(13):
        part[k] = partial[:, 128 * k : 128 * k + 128]

    def send_part(k):
        @pl.when(k != mp)
        def _():
            copy(part.at[k], part_r.at[mp], s_pr.at[k], r_pr.at[mp], dp, k).start()

        @pl.when(k == mp)
        def _():
            part_r[mp] = part[k]

    loop(0, 13, send_part)

    @pl.when(mp < 13)
    def _():
        def wait_part(k):
            @pl.when(k != mp)
            def _():
                got(part_r.at[k], r_pr.at[k])

        loop(0, 16, wait_part)
        pooled = part_r[0]
        for k in range(1, 16):
            pooled = pooled + part_r[k]
        pooled_all[mp] = (pooled + bias2[mp]).astype(BF16).astype(F32)

        def send_pooled(k):
            copy(
                pooled_all.at[mp], pooled_all.at[mp], s_pf.at[k], r_pf.at[mp], dp,
                lax.rem(mp + k, 16),
            ).start()

        loop(1, 16, send_pooled)

    def wait_pooled(k):
        @pl.when(k != mp)
        def _():
            got(pooled_all.at[k], r_pf.at[k])

    proj_copy.wait()
    loop(0, 13, wait_pooled)
    pooled = jnp.concatenate([pooled_all[k] for k in range(13)], axis=1)
    pooled_norm = layer_norm(pooled, final_gain[...].reshape(1, D))
    pooled_norm = jnp.concatenate([pooled_norm, jnp.zeros_like(pooled_norm)], axis=0).astype(BF16)
    embedding = jnp.dot(pooled_norm, proj[...], preferred_element_type=F32)[:8]
    unit = embedding * lax.rsqrt(jnp.sum(embedding * embedding, axis=1, keepdims=True) + 1e-06)
    cols = pl.ds(pl.multiple_of(640 * core, 128), 640)
    rest = pl.ds(pl.multiple_of(640 * (1 - core), 128), 640)
    unit_g[dp] = unit[:4].astype(BF16)

    def send_unit(k):
        mine = unit_g.at[dp, :, cols]
        copy(mine, mine, s_un.at[k], r_un.at[k], lax.rem(dp + k, 16), mp).start()

    loop(1, 16, send_unit)

    def wait_cls(k):
        @pl.when(k != mp)
        def _():
            got(cls.at[k], r_cl.at[k])

    @pl.when(mp < CLS_BLOCKS)
    def _():
        loop(0, 16, wait_cls)

    def wait_unit(k):
        theirs = unit_g.at[lax.rem(dp + 16 - k, 16), :, cols]
        got(theirs, r_un.at[k])
        copy(theirs, theirs, s_us.at[k], r_us.at[k], dp, sibling).start()

    loop(1, 16, wait_unit)

    def wait_rest(k):
        got(unit_g.at[lax.rem(dp + 16 - k, 16), :, rest], r_us.at[k])

    loop(1, 16, wait_rest)

    @pl.when(mp < CLS_BLOCKS)
    def _():
        lhs = unit_g[...].astype(F32).reshape(64, EMB).astype(BF16)
        rhs = jnp.concatenate([cls[k] for k in range(16)], axis=0)
        scores = jnp.dot(lhs, rhs, preferred_element_type=F32) * 100.0
        lg[...] = scores.reshape(16, 4, 128)
        lr[dp] = lg[dp]

        def send_logits(k):
            to = lax.rem(dp + k, 16)
            copy(lg.at[to], lr.at[dp], s_lg.at[k], r_lg.at[k], to, mp).start()

        loop(1, 16, send_logits)

        def wait_logits(k):
            got(lr.at[lax.rem(dp + 16 - k, 16)], r_lg.at[k])

        loop(1, 16, wait_logits)
        ob[mp] = lr[...].reshape(64, 128).astype(BF16)

        def send_ob(k):
            copy(
                ob.at[mp], ob.at[mp], s_ob.at[k], r_ob.at[mp], dp, lax.rem(chip + k, 8) * 2 + core
            ).start()

        loop(1, 8, send_ob)
        copy(ob.at[mp], ob.at[mp], s_ob2.at[mp], r_ob2.at[mp], dp, sibling).start()

    for k in range(CLS_BLOCKS):
        @pl.when(jnp.logical_and(core == k % 2, mp != k))
        def _(k=k):
            got(ob.at[k], r_ob.at[k])
            copy(ob.at[k], ob.at[k], s_ob2.at[k], r_ob2.at[k], dp, sibling).start()

    for k in range(CLS_BLOCKS):
        @pl.when(core != k % 2)
        def _(k=k):
            got(ob.at[k], r_ob2.at[k])

    ob_out[...] = ob[...]

    def sent_a2a(k):
        sent(tok.at[pl.ds(0, 17)], s_a2a.at[k])
        sent(unit_g.at[0, :, cols], s_un.at[k])
        sent(unit_g.at[0, :, cols], s_us.at[k])

    loop(1, 16, sent_a2a)

    def sent_ring(t):
        def step(n):
            sent(gath.at[t, 0], s_ring.at[t, n])

        loop(0, 15, step)

    loop(0, 4, sent_ring)
    ag_sent(0, x1)
    ag_sent(1, x2)
    for o in range(4):
        sent(p_sib.at[o, pl.ds(0, 144 if o == 3 else 128)], s_half.at[o])
    loop(0, 14, lambda n: sent(red.at[0, 0], s_rs.at[n]))

    @pl.when(extra_src)
    def _():
        sent(extra_r.at[0], s_ex.at[0, 0])

    def sent_cls(k):
        @pl.when(k != mp)
        def _():
            sent(cls.at[0], s_cl.at[k])

    loop(0, CLS_BLOCKS, sent_cls)

    def sent_part(k):
        @pl.when(k != mp)
        def _():
            sent(part.at[0], s_pr.at[k])

    loop(0, 13, sent_part)

    @pl.when(mp < 13)
    def _():
        loop(1, 16, lambda k: sent(part.at[0], s_pf.at[k]))

    @pl.when(mp < CLS_BLOCKS)
    def _():
        loop(1, 16, lambda k: sent(lg.at[0], s_lg.at[k]))
        loop(1, 8, lambda k: sent(ob.at[0], s_ob.at[k]))

    for k in range(CLS_BLOCKS):
        @pl.when(core == k % 2)
        def _(k=k):
            sent(ob.at[0], s_ob2.at[k])


def finish(labels, ob, out, lab_out):
    found = jnp.zeros((4, 128), F32)
    lane = lax.broadcasted_iota(jnp.int32, (4, 128), 1)
    row = lax.broadcasted_iota(jnp.int32, (4, 128), 0)
    label = jnp.full((4, 128), labels[0], jnp.int32)
    for i in range(1, 4):
        label = jnp.where(row == i, labels[i], label)
    for k in range(CLS_BLOCKS):
        vals = ob[k].astype(F32)
        for g in range(16):
            first = (g * CLS_BLOCKS + k) * 128
            piece = vals[4 * g : 4 * g + 4]
            out[:, first : first + 128] = piece
            found = found + jnp.where(lane + first == label, piece, 0.0)
    for i in range(4):
        lab_out[i] = jnp.sum(found[i : i + 1])


def per_device(
    tokens, up_ckpts, up_bias_ckpts, down_ckpts, down_bias_ckpts, norm_ckpts, soup_mask,
    final_gain, projection, class_embed, labels,
):
    vm = pl.BlockSpec(memory_space=pltpu.VMEM)
    sm = pl.BlockSpec(memory_space=pltpu.SMEM)
    hbm = pl.BlockSpec(memory_space=pl.ANY)
    dma = pltpu.SemaphoreType.DMA
    scores = pl.pallas_call(
        kernel,
        out_shape=jax.ShapeDtypeStruct((CLS_BLOCKS, 64, 128), BF16),
        in_specs=[sm, vm, hbm, hbm, vm, vm, vm, vm, hbm, vm],
        out_specs=vm,
        scratch_shapes=[
            pltpu.VMEM((2, CKPT, DB, FFB), BF16),
            pltpu.VMEM((2, CKPT, DB, FFB), BF16),
            pltpu.VMEM((16, 17, 4, DB), BF16),
            pltpu.VMEM((OWN, D), F32),
            pltpu.VMEM((ROWS, D), BF16),
            pltpu.VMEM((ROWS, D), BF16),
            pltpu.VMEM((4, 16, 2 * DB, 256), BF16),
            pltpu.VMEM((D, FFB), BF16),
            pltpu.VMEM((D, FFB), BF16),
            pltpu.VMEM((D, FFB), BF16),
            pltpu.VMEM((D, FFB), BF16),
            pltpu.VMEM((ROWS, FFB), BF16),
            pltpu.VMEM((4, 144, D), BF16),
            pltpu.VMEM((4, 144, D), BF16),
            pltpu.VMEM((4, 144, D), BF16),
            pltpu.VMEM((7, 2, 32, D), BF16),
            pltpu.VMEM((16, D), F32),
            pltpu.VMEM((8, 16, D), BF16),
            pltpu.VMEM((13, 8, 128), F32),
            pltpu.VMEM((16, 8, 128), F32),
            pltpu.VMEM((13, 8, 128), F32),
            pltpu.VMEM((13, 8, 128), F32),
            pltpu.VMEM((D, EMB), BF16),
            pltpu.VMEM((16, 4, EMB), BF16),
            pltpu.VMEM((16, EMBB, 128), BF16),
            pltpu.VMEM((16, 4, 128), F32),
            pltpu.VMEM((16, 4, 128), F32),
            pltpu.VMEM((CLS_BLOCKS, 64, 128), BF16),
            dma((16,)), dma((16,)),
            dma((2, 14)), dma((2, 14)),
            dma((2, 17)), dma((2, 17)),
            dma((4, 15)), dma((4, 15)),
            dma((14,)), dma((14,)),
            dma((4,)), dma((4,)),
            dma((2, 8)), dma((10,)),
            dma((16,)), dma((16,)),
            dma((16,)), dma((16,)),
            dma((16,)), dma((16,)),
            dma((16,)), dma((16,)),
            dma((16,)), dma((16,)),
            dma((16,)), dma((16,)),
            dma((8,)), dma((16,)),
            dma((16,)), dma((16,)),
            dma(()),
            dma((4,)),
        ],
        compiler_params=pltpu.CompilerParams(
            collective_id=0, has_side_effects=True, vmem_limit_bytes=60 * 2**20
        ),
    )(
        soup_mask, jnp.swapaxes(tokens, 0, 1), up_ckpts, jnp.swapaxes(down_ckpts, 2, 3),
        jnp.swapaxes(up_bias_ckpts, 0, 1), jnp.swapaxes(down_bias_ckpts, 0, 1),
        jnp.swapaxes(norm_ckpts, 0, 1), final_gain, projection, class_embed.T,
    )
    return pl.pallas_call(
        finish,
        out_shape=(
            jax.ShapeDtypeStruct((4, 16 * CLS_BLOCKS * 128), F32),
            jax.ShapeDtypeStruct((4,), F32),
        ),
        in_specs=[sm, vm],
        out_specs=(vm, sm),
    )(labels, scores)


def solution(mesh):
    placed = (
        P("dp", None, "mp"),
        P(None, None, "dp", "mp"),
        P(None, None, "mp"),
        P(None, None, "mp", "dp"),
        P(),
        P(),
        P(),
        P(),
        P(),
        P("dp", "mp"),
        P("dp"),
    )
    return jax.shard_map(
        per_device, mesh=mesh, in_specs=placed, out_specs=(P("dp", None), P("dp")), check_vma=False
    )
```

time: 196 us -> 140 us (0.71)
  Pallas kernels: 180 us -> 139 us
  local copies, waits for them, and re-layouts: 14.9 us -> 0 us
    pallas_call x1 -> x2, Pallas kernels: 180 us -> 139 us  [the longest x1 137 us: per_device(): pl.pallas_call(kernel, out_shape=jax.ShapeDtypeStruct((CLS_BLOCKS, 64, 12...]
    unnamed x8 -> x0, local copies, waits for them, and re-layouts: 9.94 us -> none
    broadcast_in_dim x2 -> x0, local copies, waits for them, and re-layouts: 2.77 us -> none  [the longest x1 1.48 us: per_device(): labels[:, None]]
where the time goes in v2:
time: 140 us
  Pallas kernels  139 us (99%)
    pallas_call x1, Pallas kernels, per_device(): pl.pallas_call(kernel, out_shape=jax.ShapeDtypeStruct((CLS_BLOCKS, 64, 12...  137 us

profile of v2, /device:TPU:1, one launch (start us, length us, event | category | flops | bytes accessed | tf_op | source)
XLA Modules:
  0.0 139.7 jit_solution(1621850481683552268)
XLA Ops:
  0.6 137.2 %shard_map.122.ob = bf16[11,64,128]{2,1,0:T(8,128)(2,1)} custom-call(s32[10]{0:T(128)} %mask.1, bf16[257,4,104]{2,1,0:T(4,128)(2,1)} %bitcast.7, bf16[2,10,104,512]{3,2,1,0:T(8,128)(2,1)} %up_hbm.1, bf16[2,10,104,512]{3,2,1,0:T(8,128)(2,1)} %bitcast.6, f32[10,2,512]{2,1,0:T(2,128)} %bitcast.11, f32[10,2,1664]{2,1,0:T(2,128)} %bitcast.9, ...), custom_call_target="tpu_custom_call" | custom-call | tf_op jit(solution)/shard_map/pallas_call | solution.py:703
  137.8 1.9 %shard_map.123 = (f32[4,22528]{1,0:T(4,128)}, f32[4]{0:T(128)}) custom-call(s32[4]{0:T(128)} %labels.1, bf16[11,64,128]{2,1,0:T(8,128)(2,1)} %shard_map.122.ob), custom_call_target="tpu_custom_call" | custom-call | tf_op jit(solution)/shard_map/pallas_call | solution.py:763

commit v3 on v2

--- a/solution.py
+++ b/solution.py
@@ -24,6 +24,7 @@
 CLS_BLOCKS = 11
 UP1, DOWN1, UP2, DOWN2 = 0, 1, 2, 3
 PLACES = ((-1, 0), (1, 0), (0, 1), (-1, 1), (1, 1), (2, 0), (2, 1), (0, 0))
+FAR = (0, -1, 1, -2, 2, -3, 3, 4)
 STEPS = (2, -1, 1, 0)
 
 
@@ -38,13 +39,13 @@
 
 
 def kernel(
-    mask, tok, up_hbm, down_hbm, up_b, down_b, norm_g, final_gain, proj_hbm, cet,
+    mask, tok_hbm, up_hbm, down_hbm, up_b_hbm, down_b_hbm, norm_hbm, final_hbm, proj_hbm, cet_hbm,
     ob_out,
-    up_ck, down_ck, a2a, state, x1, x2, gath, w_up1, w_dn1, w_up2, w_dn2, hid, p_sib, s_sib, t_own,
-    red, extra_s, extra_r, part, part_r, pooled_all, bias2, proj, unit_g, cls, lg, lr, ob,
-    s_a2a, r_a2a, s_ag, r_ag, s_sb, r_sb, s_ring, r_ring, s_rs, r_rs, s_half, r_half, s_ex, r_ex,
-    s_pr, r_pr, s_pf, r_pf, s_cl, r_cl, s_un, r_un, s_us, r_us, s_lg, r_lg, s_ob, r_ob, s_ob2, r_ob2,
-    proj_sem, ck_sem,
+    up_ck, down_ck, tok, up_b, down_b, norm_g, final_gain, cet, a2a, state, x1, x2, gath, w_up1, w_dn1, w_up2, w_dn2, hid, p_sib, s_sib, t_own,
+    red, extra_r, part, part_r, pair, proj, unit_m, unit_r, cls, lg, lr, ob,
+    s_a2a, r_a2a, s_ag, r_ag, s_sb, r_sb, s_ring, r_ring, s_far, r_far, s_rs, r_rs, s_half, r_half, s_ex, r_ex,
+    s_pr, r_pr, s_cl, r_cl, s_un, r_un, s_lg, r_lg, s_ob, r_ob,
+    ck_sem,
 ):
     dp = lax.axis_index("dp")
     mp = lax.axis_index("mp")
@@ -88,13 +89,23 @@
             ((up_hbm, up_ck, 0), (down_hbm, down_ck, 0), (up_hbm, up_ck, 1), (down_hbm, down_ck, 1))
         )
     ]
+    tok_load, norm_load, up_b_load, cet_load, down_b_load, final_load, proj_load = (
+        pltpu.make_async_copy(src, dst, ck_sem.at[4 + n])
+        for n, (src, dst) in enumerate(
+            (
+                (tok_hbm, tok), (norm_hbm, norm_g), (up_b_hbm, up_b), (cet_hbm, cet),
+                (down_b_hbm, down_b), (final_hbm, final_gain), (proj_hbm, proj),
+            )
+        )
+    )
+    tok_load.start()
     for load in loads:
         load.start()
-    proj_copy = pltpu.make_async_copy(proj_hbm, proj, proj_sem)
-    proj_copy.start()
+    for load in (norm_load, up_b_load, cet_load, down_b_load, final_load, proj_load):
+        load.start()
 
     state[64:80, :] = jnp.zeros((16, D), F32)
-    extra_r[...] = jnp.zeros((8, 16, D), BF16)
+    ob[1, 5] = jnp.zeros((64, 128), BF16)
     barrier = pltpu.get_barrier_semaphore()
 
     def greet(k):
@@ -144,8 +155,9 @@
         got(gath.at[t, s], r_ring.at[t, n])
 
     def ring(t, step):
-        if step == 0:
+        if step == 9:
             ring_push(t, dp, 14, other_yh * 8 + z)
+        elif step == 0:
             ring_push(t, dp, 0, z_next)
             ring_push(t, dp, 7, z_prev)
         elif step == 1:
@@ -170,6 +182,34 @@
             ring_got(t, slot(yh, 4), 6)
             ring_got(t, slot(other_yh, 4), 13)
 
+    def far_across(t, k):
+        s = slot(yh, FAR[k])
+        copy(
+            gath.at[t, s], gath.at[t, s], s_far.at[k], r_far.at[k], other_yh * 8 + z, mp
+        ).start()
+
+    def far_ring(t, step):
+        if step == 0:
+            ring_push(t, dp, 0, z_next)
+            ring_push(t, dp, 7, z_prev)
+        elif step < 4:
+            sl, sr = slot(yh, -step), slot(yh, step)
+            ring_got(t, sl, step - 1)
+            ring_push(t, sl, step, z_next)
+            ring_got(t, sr, 7 + step - 1)
+            if step < 3:
+                ring_push(t, sr, 7 + step, z_prev)
+            if step == 1:
+                far_across(t, 0)
+            far_across(t, 2 * step - 1)
+            far_across(t, 2 * step)
+        elif step == 4:
+            ring_got(t, slot(yh, 4), 3)
+            far_across(t, 7)
+        else:
+            for k in range(8):
+                got(gath.at[t, slot(other_yh, FAR[k])], r_far.at[k])
+
     def compact(t, dst):
         def pair(j):
             g0 = gath[t, 2 * j].astype(F32)
@@ -198,13 +238,13 @@
         n = 2 * idx + h
         copy(rows, rows, s_sb.at[lay, n], r_sb.at[lay, n], dp, sibling).start()
 
-    def ag_start(lay, x):
-        for h in range(2):
-            ag_push(lay, x, 7, 0, h, right)
-            ag_push(lay, x, 7, 1, h, left)
-            ag_push(lay, x, 7, 2, h, across)
-        for h in range(2):
-            ag_sib(lay, x, 7, h)
+    def ag_start(lay, x, h):
+        ag_push(lay, x, 7, 0, h, right)
+        ag_push(lay, x, 7, 1, h, left)
+        ag_push(lay, x, 7, 2, h, across)
+        ag_sib(lay, x, 7, h)
+
+    def ag_start_extra(lay, x):
         extra = x.at[pl.ds(1024, 16)]
 
         @pl.when(last)
@@ -219,13 +259,14 @@
 
     def ag_recv(lay, x, idx, h):
         got(half_rows(x, core, idx, h), r_ag.at[lay, 2 * idx + h])
+        by_y = lay == 1 and h == 1
         if idx == 0:
             ag_push(lay, x, 0, 5, h, right)
-            if h == 1:
+            if by_y:
                 ag_push(lay, x, 0, 3, h, across)
-        elif idx == 1 and h == 1:
+        elif idx == 1 and by_y:
             ag_push(lay, x, 1, 4, h, across)
-        elif idx == 2 and h == 0:
+        elif idx == 2 and not by_y:
             ag_push(lay, x, 2, 3, h, right)
             ag_push(lay, x, 2, 4, h, left)
         elif idx == 4:
@@ -296,6 +337,7 @@
         rows[...] = acc.astype(BF16)
 
     own_shard(UP1, up_ck, 0)
+    tok_load.wait()
     pl.semaphore_wait(barrier, 30)
 
     def send_tokens(k):
@@ -305,12 +347,13 @@
         copy(src, a2a.at[mp], s_a2a.at[k], r_a2a.at[k], dp, m2).start()
 
     loop(1, 16, send_tokens)
+    ring(UP1, 9)
     ring(UP1, 0)
     a2a[mp] = tok[pl.ds(16 * block, 17)]
     own_shard(DOWN1, down_ck, 0)
-    ring(DOWN1, 0)
+    far_ring(DOWN1, 0)
+    norm_load.wait()
     gain1 = soup_vec(norm_g, 0, D)
-    ring(UP1, 1)
 
     def wait_tokens(k):
         got(a2a.at[lax.rem(mp + 16 - k, 16)], r_a2a.at[k])
@@ -319,43 +362,47 @@
     for j in range(16):
         state[:68, DB * j : DB * j + DB] = a2a[j].astype(F32).reshape(68, DB)
     normed_rows(x1, gain1)
-    ag_start(0, x1)
+    ag_start(0, x1, 0)
+    ag_start(0, x1, 1)
+    ag_start_extra(0, x1)
+    ring(UP1, 1)
     ring(UP1, 2)
     own_shard(UP2, up_ck, 1)
+    far_ring(DOWN1, 1)
     ring(UP1, 3)
     for idx in range(3):
         ag_recv(0, x1, idx, 0)
     ring(UP1, 4)
     for idx in range(3):
         ag_recv(0, x1, idx, 1)
+    far_ring(DOWN1, 2)
     ring(UP1, 5)
     ag_recv(0, x1, 3, 0)
     ag_recv(0, x1, 4, 0)
     ring(UP1, 6)
-    ring(DOWN1, 1)
+    far_ring(DOWN1, 3)
     ag_recv(0, x1, 3, 1)
     ag_recv(0, x1, 4, 1)
     ag_recv(0, x1, 5, 0)
     ring(UP1, 7)
-    ring(DOWN1, 2)
     ag_recv(0, x1, 5, 1)
     ag_recv(0, x1, 6, 0)
+    far_ring(DOWN1, 4)
     ag_recv(0, x1, 6, 1)
     ag_extra(0, x1)
     own_shard(DOWN2, down_ck, 1)
     ring(UP1, 8)
-    ring(DOWN1, 3)
+    ring(UP2, 0)
     compact(UP1, w_up1)
+    up_b_load.wait()
     bias_up1 = soup_vec(up_b, 0, FFB)
     ag_finish(0, x1)
     for ch in range(5):
         hid[CHUNK * ch : CHUNK * ch + CHUNK, :] = up_chunk(x1, w_up1, bias_up1, ch)
-        if ch == 0:
-            ring(DOWN1, 4)
-        if ch == 2:
-            ring(DOWN1, 5)
-        if ch == 4:
-            ring(DOWN1, 6)
+        if ch == 1:
+            ring(UP2, 9)
+        if ch == 3:
+            ring(UP2, 2)
 
     def send_cls(k):
         @pl.when(k != mp)
@@ -367,52 +414,69 @@
         def _():
             cls[mp] = cet[:, pl.ds(pl.multiple_of(128 * k, 128), 128)]
 
+    cet_load.wait()
     loop(0, CLS_BLOCKS, send_cls)
+    down_b_load.wait()
     gain2 = soup_vec(norm_g, 1, D)
     bias_down1 = soup_vec(down_b, 0, D)
     bias_up2 = soup_vec(up_b, 1, FFB)
     bias_down2 = soup_vec(down_b, 1, D)
-    for k in range(13):
-        bias2[k] = jnp.broadcast_to(bias_down2[:, 128 * k : 128 * k + 128], (8, 128))
-    ring(DOWN1, 7)
-    ring(UP2, 0)
+    far_ring(DOWN1, 5)
     ring(UP2, 1)
-    ring(DOWN1, 8)
     compact(DOWN1, w_dn1)
 
+    def chunk_product(o, c):
+        lhs = hid[pl.ds(block_rows(c, STEPS[o], 0), 128), :]
+        if STEPS[o] == 0:
+            lhs = jnp.concatenate([lhs, hid[1024:1040, :]], axis=0)
+        return down_product(lhs)
+
+    def chunk_rows(o):
+        return pl.ds(0, 144 if STEPS[o] == 0 else 128)
+
+    def sib_chunk(o):
+        rows = chunk_rows(o)
+        p_sib[o, rows, :] = chunk_product(o, 1 - core).astype(BF16)
+        copy(p_sib.at[o, rows], s_sib.at[o, rows], s_half.at[o], r_half.at[o], dp, sibling).start()
+
     def own_chunk(o):
-        dx = STEPS[o]
-        size = 144 if dx == 0 else 128
-        rows = pl.ds(0, size)
-        for c in (1 - core, core):
-            lhs = hid[pl.ds(block_rows(c, dx, 0), 128), :]
-            if dx == 0:
-                lhs = jnp.concatenate([lhs, hid[1024:1040, :]], axis=0)
-            term = down_product(lhs)
-            if c is not core:
-                p_sib[o, rows, :] = term.astype(BF16)
-                copy(
-                    p_sib.at[o, rows], s_sib.at[o, rows], s_half.at[o], r_half.at[o], dp, sibling
-                ).start()
+        rows = chunk_rows(o)
+        term = chunk_product(o, core)
         got(s_sib.at[o, rows], r_half.at[o])
         t_own[o, rows, :] = (term + s_sib[o, rows, :].astype(F32)).astype(BF16)
 
+    def finish_half(h):
+        rs_add(3, yl, h, 4, 5, 6)
+        part_rows = slice(32 * h, 32 * h + 32)
+        new = state[part_rows, :] + bias_down1 + rs_rows(3, yl, h)[...].astype(F32)
+        new = new.astype(BF16).astype(F32)
+        state[part_rows, :] = new
+        x2[pl.ds(block_rows(core, 0, yl) + 32 * h, 32), :] = layer_norm(new, gain2).astype(BF16)
+        ag_start(1, x2, h)
+
+    sib_chunk(0)
+    sib_chunk(1)
     own_chunk(0)
     for h in range(2):
         rs_push(0, yl, 0, h, left)
         rs_push(0, 1 - yl, 1, h, right)
+    ring(UP2, 3)
+    sib_chunk(2)
     own_chunk(1)
-    for h in range(2):
-        rs_push(1, 1 - yl, 2, h, left)
+    rs_push(1, 1 - yl, 2, 0, left)
+    rs_push(1, 1 - yl, 2, 1, left)
+    ring(UP2, 4)
+    sib_chunk(3)
     own_chunk(2)
     for h in range(2):
         rs_add(2, 1 - yl, h, 1)
         rs_push(2, 1 - yl, 3, h, right)
+    ring(UP2, 5)
+    for h in range(2):
         rs_add(1, yl, h, 0)
         rs_push(1, yl, 4, h, left)
-    for h in range(2):
         rs_push(2, yl, 5, h, right)
-    ring(UP2, 2)
+    ring(UP2, 6)
     own_chunk(3)
 
     @pl.when(extra_src)
@@ -421,16 +485,17 @@
             t_own.at[3, pl.ds(128, 16)], extra_r.at[chip], s_ex.at[0, 0], r_ex.at[2 + chip], dp, 15
         ).start()
 
-    ring(UP2, 3)
+    rs_add(3, 1 - yl, 0, 3, 2)
+    rs_push(3, 1 - yl, 6, 0, across)
+    ring(UP2, 7)
     ring(DOWN2, 0)
-    for h in range(2):
-        rs_add(3, 1 - yl, h, 3, 2)
-        rs_push(3, 1 - yl, 6, h, across)
-    ring(UP2, 4)
-    ring(UP2, 5)
-    ring(DOWN2, 1)
-    for h in range(2):
-        rs_add(3, yl, h, 4, 5, 6)
+    rs_add(3, 1 - yl, 1, 3, 2)
+    rs_push(3, 1 - yl, 6, 1, across)
+    ring(UP2, 8)
+    ring(DOWN2, 9)
+    finish_half(0)
+    ring(DOWN2, 2)
+    finish_half(1)
 
     @pl.when(last)
     def _():
@@ -438,19 +503,11 @@
         for q in range(7):
             got(extra_r.at[q], r_ex.at[2 + q])
             extra = extra + extra_r[q].astype(F32)
-        extra_s[...] = extra
-
-    @pl.when(jnp.logical_not(last))
-    def _():
-        extra_s[...] = jnp.zeros((16, D), F32)
-
-    summed = jnp.concatenate(
-        [t_own[3, pl.ds(pl.multiple_of(64 * yl, 16), 64), :].astype(F32), extra_s[...]], axis=0
-    )
-    state[...] = (state[...] + bias_down1 + summed).astype(BF16).astype(F32)
-    normed_rows(x2, gain2)
-    ag_start(1, x2)
-    ring(UP2, 6)
+        extra = (state[64:80, :] + bias_down1 + extra).astype(BF16).astype(F32)
+        state[64:80, :] = extra
+        x2[1024:1040, :] = layer_norm(extra, gain2).astype(BF16)
+
+    ag_start_extra(1, x2)
 
     row = lax.broadcasted_iota(jnp.int32, (16, OWN), 1)
     img = lax.broadcasted_iota(jnp.int32, (16, OWN), 0)
@@ -458,27 +515,26 @@
     state_sum = jnp.dot(
         jnp.where(inside, 1.0, 0.0).astype(BF16), state[...].astype(BF16), preferred_element_type=F32
     )[:8]
-    ring(UP2, 7)
-    ring(DOWN2, 2)
+    ring(DOWN2, 1)
+    ring(DOWN2, 3)
     for idx in range(3):
         ag_recv(1, x2, idx, 0)
-    ring(UP2, 8)
+    compact(UP2, w_up2)
+    ring(DOWN2, 4)
     for idx in range(3):
         ag_recv(1, x2, idx, 1)
-    ring(DOWN2, 3)
+    ring(DOWN2, 5)
     ag_recv(1, x2, 3, 0)
     ag_recv(1, x2, 4, 0)
-    ring(DOWN2, 4)
-    compact(UP2, w_up2)
+    ag_recv(1, x2, 5, 0)
+    ring(DOWN2, 6)
     ag_recv(1, x2, 3, 1)
     ag_recv(1, x2, 4, 1)
-    ag_recv(1, x2, 5, 0)
-    ring(DOWN2, 5)
+    ag_recv(1, x2, 6, 0)
+    ring(DOWN2, 7)
     ag_recv(1, x2, 5, 1)
-    ag_recv(1, x2, 6, 0)
     ag_recv(1, x2, 6, 1)
     ag_extra(1, x2)
-    ring(DOWN2, 6)
     ag_finish(1, x2)
     hsum = jnp.zeros((16, FFB), F32)
     for ch in range(5):
@@ -489,8 +545,6 @@
         hsum = hsum + jnp.dot(
             jnp.where(inside, 1.0, 0.0).astype(BF16), h, preferred_element_type=F32
         )
-        if ch == 1:
-            ring(DOWN2, 7)
     ring(DOWN2, 8)
     compact(DOWN2, w_dn2)
 
@@ -502,131 +556,39 @@
         (((1,), (1,)), ((), ())), preferred_element_type=F32,
     )
     partial = both[:8] + both[8:] + state_sum * (1.0 / TOKS)
-    for k in range(13):
-        part[k] = partial[:, 128 * k : 128 * k + 128]
-
-    def send_part(k):
-        @pl.when(k != mp)
-        def _():
-            copy(part.at[k], part_r.at[mp], s_pr.at[k], r_pr.at[mp], dp, k).start()
-
-        @pl.when(k == mp)
-        def _():
-            part_r[mp] = part[k]
-
-    loop(0, 13, send_part)
-
-    @pl.when(mp < 13)
-    def _():
-        def wait_part(k):
-            @pl.when(k != mp)
-            def _():
-                got(part_r.at[k], r_pr.at[k])
-
-        loop(0, 16, wait_part)
-        pooled = part_r[0]
-        for k in range(1, 16):
-            pooled = pooled + part_r[k]
-        pooled_all[mp] = (pooled + bias2[mp]).astype(BF16).astype(F32)
-
-        def send_pooled(k):
-            copy(
-                pooled_all.at[mp], pooled_all.at[mp], s_pf.at[k], r_pf.at[mp], dp,
-                lax.rem(mp + k, 16),
-            ).start()
-
-        loop(1, 16, send_pooled)
-
-    def wait_pooled(k):
-        @pl.when(k != mp)
-        def _():
-            got(pooled_all.at[k], r_pf.at[k])
-
-    proj_copy.wait()
-    loop(0, 13, wait_pooled)
-    pooled = jnp.concatenate([pooled_all[k] for k in range(13)], axis=1)
+    part[...] = partial[:4]
+    copy(part, part_r, s_pr.at[0], r_pr.at[0], dp, sibling).start()
+    got(part_r, r_pr.at[0])
+    pair[chip] = (part[...] + part_r[...]).astype(BF16)
+
+    def send_pair(k):
+        copy(
+            pair.at[chip], pair.at[chip], s_pr.at[k], r_pr.at[k], dp, lax.rem(chip + k, 8) * 2 + core
+        ).start()
+
+    loop(1, 8, send_pair)
+    final_load.wait()
+    proj_load.wait()
+    loop(1, 8, lambda k: got(pair.at[lax.rem(chip + 8 - k, 8)], r_pr.at[k]))
+    pooled = pair[0].astype(F32)
+    for k in range(1, 8):
+        pooled = pooled + pair[k].astype(F32)
+    pooled = (pooled + bias_down2).astype(BF16).astype(F32)
+    pooled = jnp.concatenate([pooled, jnp.zeros_like(pooled)], axis=0)
     pooled_norm = layer_norm(pooled, final_gain[...].reshape(1, D))
     pooled_norm = jnp.concatenate([pooled_norm, jnp.zeros_like(pooled_norm)], axis=0).astype(BF16)
     embedding = jnp.dot(pooled_norm, proj[...], preferred_element_type=F32)[:8]
     unit = embedding * lax.rsqrt(jnp.sum(embedding * embedding, axis=1, keepdims=True) + 1e-06)
-    cols = pl.ds(pl.multiple_of(640 * core, 128), 640)
-    rest = pl.ds(pl.multiple_of(640 * (1 - core), 128), 640)
-    unit_g[dp] = unit[:4].astype(BF16)
+    first_core = core == 0
+    unit_m[dp] = jnp.where(first_core, unit[:4, :640], unit[:4, 640:]).astype(BF16)
 
     def send_unit(k):
-        mine = unit_g.at[dp, :, cols]
+        mine = unit_m.at[dp]
         copy(mine, mine, s_un.at[k], r_un.at[k], lax.rem(dp + k, 16), mp).start()
 
     loop(1, 16, send_unit)
 
-    def wait_cls(k):
-        @pl.when(k != mp)
-        def _():
-            got(cls.at[k], r_cl.at[k])
-
-    @pl.when(mp < CLS_BLOCKS)
-    def _():
-        loop(0, 16, wait_cls)
-
-    def wait_unit(k):
-        theirs = unit_g.at[lax.rem(dp + 16 - k, 16), :, cols]
-        got(theirs, r_un.at[k])
-        copy(theirs, theirs, s_us.at[k], r_us.at[k], dp, sibling).start()
-
-    loop(1, 16, wait_unit)
-
-    def wait_rest(k):
-        got(unit_g.at[lax.rem(dp + 16 - k, 16), :, rest], r_us.at[k])
-
-    loop(1, 16, wait_rest)
-
-    @pl.when(mp < CLS_BLOCKS)
-    def _():
-        lhs = unit_g[...].astype(F32).reshape(64, EMB).astype(BF16)
-        rhs = jnp.concatenate([cls[k] for k in range(16)], axis=0)
-        scores = jnp.dot(lhs, rhs, preferred_element_type=F32) * 100.0
-        lg[...] = scores.reshape(16, 4, 128)
-        lr[dp] = lg[dp]
-
-        def send_logits(k):
-            to = lax.rem(dp + k, 16)
-            copy(lg.at[to], lr.at[dp], s_lg.at[k], r_lg.at[k], to, mp).start()
-
-        loop(1, 16, send_logits)
-
-        def wait_logits(k):
-            got(lr.at[lax.rem(dp + 16 - k, 16)], r_lg.at[k])
-
-        loop(1, 16, wait_logits)
-        ob[mp] = lr[...].reshape(64, 128).astype(BF16)
-
-        def send_ob(k):
-            copy(
-                ob.at[mp], ob.at[mp], s_ob.at[k], r_ob.at[mp], dp, lax.rem(chip + k, 8) * 2 + core
-            ).start()
-
-        loop(1, 8, send_ob)
-        copy(ob.at[mp], ob.at[mp], s_ob2.at[mp], r_ob2.at[mp], dp, sibling).start()
-
-    for k in range(CLS_BLOCKS):
-        @pl.when(jnp.logical_and(core == k % 2, mp != k))
-        def _(k=k):
-            got(ob.at[k], r_ob.at[k])
-            copy(ob.at[k], ob.at[k], s_ob2.at[k], r_ob2.at[k], dp, sibling).start()
-
-    for k in range(CLS_BLOCKS):
-        @pl.when(core != k % 2)
-        def _(k=k):
-            got(ob.at[k], r_ob2.at[k])
-
-    ob_out[...] = ob[...]
-
-    def sent_a2a(k):
-        sent(tok.at[pl.ds(0, 17)], s_a2a.at[k])
-        sent(unit_g.at[0, :, cols], s_un.at[k])
-        sent(unit_g.at[0, :, cols], s_us.at[k])
-
-    loop(1, 16, sent_a2a)
+    loop(1, 16, lambda k: sent(tok.at[pl.ds(0, 17)], s_a2a.at[k]))
 
     def sent_ring(t):
         def step(n):
@@ -634,7 +596,11 @@
 
         loop(0, 15, step)
 
-    loop(0, 4, sent_ring)
+    for t in (UP1, UP2, DOWN2):
+        sent_ring(t)
+    loop(0, 4, lambda n: sent(gath.at[0, 0], s_ring.at[DOWN1, n]))
+    loop(7, 10, lambda n: sent(gath.at[0, 0], s_ring.at[DOWN1, n]))
+    loop(0, 8, lambda n: sent(gath.at[0, 0], s_far.at[n]))
     ag_sent(0, x1)
     ag_sent(1, x2)
     for o in range(4):
@@ -652,26 +618,70 @@
 
     loop(0, CLS_BLOCKS, sent_cls)
 
-    def sent_part(k):
+
+    def wait_cls(k):
         @pl.when(k != mp)
         def _():
-            sent(part.at[0], s_pr.at[k])
-
-    loop(0, 13, sent_part)
-
-    @pl.when(mp < 13)
+            got(cls.at[k], r_cl.at[k])
+
+    @pl.when(mp < CLS_BLOCKS)
     def _():
-        loop(1, 16, lambda k: sent(part.at[0], s_pf.at[k]))
+        loop(0, 16, wait_cls)
+
+    loop(1, 16, lambda k: got(unit_m.at[lax.rem(dp + 16 - k, 16)], r_un.at[k]))
+    copy(unit_m, unit_r, s_un.at[0], r_un.at[0], dp, sibling).start()
+    got(unit_r, r_un.at[0])
+
+    @pl.when(mp < CLS_BLOCKS)
+    def _():
+        mine = unit_m[...].astype(F32).reshape(64, 640)
+        rest = unit_r[...].astype(F32).reshape(64, 640)
+        lhs = jnp.concatenate(
+            [jnp.where(first_core, mine, rest), jnp.where(first_core, rest, mine)], axis=1
+        ).astype(BF16)
+        rhs = jnp.concatenate([cls[k] for k in range(16)], axis=0)
+        scores = jnp.dot(lhs, rhs, preferred_element_type=F32) * 100.0
+        lg[...] = scores.reshape(16, 4, 128)
+        lr[dp] = lg[dp]
+
+        def send_logits(k):
+            to = lax.rem(dp + k, 16)
+            copy(lg.at[to], lr.at[dp], s_lg.at[k], r_lg.at[k], to, mp).start()
+
+        loop(1, 16, send_logits)
+
+        def wait_logits(k):
+            got(lr.at[lax.rem(dp + 16 - k, 16)], r_lg.at[k])
+
+        loop(1, 16, wait_logits)
+        ob[core, chip] = lr[...].reshape(64, 128).astype(BF16)
+
+        def send_ob(k):
+            mine = ob.at[core, chip]
+            copy(mine, mine, s_ob.at[k], r_ob.at[chip], dp, lax.rem(chip + k, 8) * 2 + core).start()
+
+        loop(1, 8, send_ob)
+
+    for k in range(6):
+        @pl.when(jnp.logical_and(chip != k, 2 * k + core < CLS_BLOCKS))
+        def _(k=k):
+            got(ob.at[core, k], r_ob.at[k])
+
+    copy(ob.at[core], ob.at[core], s_ob.at[0], r_ob.at[8], dp, sibling).start()
+    got(ob.at[1 - core], r_ob.at[8])
+    ob_out[...] = ob[...]
+
+    loop(1, 16, lambda k: sent(unit_m.at[0], s_un.at[k]))
+    sent(unit_m, s_un.at[0])
+    sent(part, s_pr.at[0])
+    loop(1, 8, lambda k: sent(pair.at[0], s_pr.at[k]))
 
     @pl.when(mp < CLS_BLOCKS)
     def _():
         loop(1, 16, lambda k: sent(lg.at[0], s_lg.at[k]))
-        loop(1, 8, lambda k: sent(ob.at[0], s_ob.at[k]))
-
-    for k in range(CLS_BLOCKS):
-        @pl.when(core == k % 2)
-        def _(k=k):
-            sent(ob.at[0], s_ob2.at[k])
+        loop(1, 8, lambda k: sent(ob.at[0, 0], s_ob.at[k]))
+
+    sent(ob.at[0], s_ob.at[0])
 
 
 def finish(labels, ob, out, lab_out):
@@ -682,7 +692,7 @@
     for i in range(1, 4):
         label = jnp.where(row == i, labels[i], label)
     for k in range(CLS_BLOCKS):
-        vals = ob[k].astype(F32)
+        vals = ob[k % 2, k // 2].astype(F32)
         for g in range(16):
             first = (g * CLS_BLOCKS + k) * 128
             piece = vals[4 * g : 4 * g + 4]
@@ -702,12 +712,18 @@
     dma = pltpu.SemaphoreType.DMA
     scores = pl.pallas_call(
         kernel,
-        out_shape=jax.ShapeDtypeStruct((CLS_BLOCKS, 64, 128), BF16),
-        in_specs=[sm, vm, hbm, hbm, vm, vm, vm, vm, hbm, vm],
+        out_shape=jax.ShapeDtypeStruct((2, 6, 64, 128), BF16),
+        in_specs=[sm] + [hbm] * 9,
         out_specs=vm,
         scratch_shapes=[
             pltpu.VMEM((2, CKPT, DB, FFB), BF16),
             pltpu.VMEM((2, CKPT, DB, FFB), BF16),
+            pltpu.VMEM((TOKS, 4, DB), BF16),
+            pltpu.VMEM((CKPT, 2, FFB), F32),
+            pltpu.VMEM((CKPT, 2, D), F32),
+            pltpu.VMEM((CKPT, 2, D), F32),
+            pltpu.VMEM((D,), F32),
+            pltpu.VMEM((EMBB, CLS_BLOCKS * 128), BF16),
             pltpu.VMEM((16, 17, 4, DB), BF16),
             pltpu.VMEM((OWN, D), F32),
             pltpu.VMEM((ROWS, D), BF16),
@@ -722,35 +738,31 @@
             pltpu.VMEM((4, 144, D), BF16),
             pltpu.VMEM((4, 144, D), BF16),
             pltpu.VMEM((7, 2, 32, D), BF16),
-            pltpu.VMEM((16, D), F32),
             pltpu.VMEM((8, 16, D), BF16),
-            pltpu.VMEM((13, 8, 128), F32),
-            pltpu.VMEM((16, 8, 128), F32),
-            pltpu.VMEM((13, 8, 128), F32),
-            pltpu.VMEM((13, 8, 128), F32),
+            pltpu.VMEM((4, D), F32),
+            pltpu.VMEM((4, D), F32),
+            pltpu.VMEM((8, 4, D), BF16),
             pltpu.VMEM((D, EMB), BF16),
-            pltpu.VMEM((16, 4, EMB), BF16),
+            pltpu.VMEM((16, 4, EMB // 2), BF16),
+            pltpu.VMEM((16, 4, EMB // 2), BF16),
             pltpu.VMEM((16, EMBB, 128), BF16),
             pltpu.VMEM((16, 4, 128), F32),
             pltpu.VMEM((16, 4, 128), F32),
-            pltpu.VMEM((CLS_BLOCKS, 64, 128), BF16),
+            pltpu.VMEM((2, 6, 64, 128), BF16),
             dma((16,)), dma((16,)),
             dma((2, 14)), dma((2, 14)),
             dma((2, 17)), dma((2, 17)),
             dma((4, 15)), dma((4, 15)),
+            dma((8,)), dma((8,)),
             dma((14,)), dma((14,)),
             dma((4,)), dma((4,)),
             dma((2, 8)), dma((10,)),
+            dma((8,)), dma((8,)),
             dma((16,)), dma((16,)),
             dma((16,)), dma((16,)),
             dma((16,)), dma((16,)),
-            dma((16,)), dma((16,)),
-            dma((16,)), dma((16,)),
-            dma((16,)), dma((16,)),
-            dma((8,)), dma((16,)),
-            dma((16,)), dma((16,)),
-            dma(()),
-            dma((4,)),
+            dma((8,)), dma((9,)),
+            dma((11,)),
         ],
         compiler_params=pltpu.CompilerParams(
             collective_id=0, has_side_effects=True, vmem_limit_bytes=60 * 2**20

time: 140 us -> 128 us (0.914)
  Pallas kernels: 139 us -> 128 us
    pallas_call x1, Pallas kernels: 137 us -> 126 us  [per_device(): pl.pallas_call(kernel, out_shape=jax.ShapeDtypeStruct((2, 6, 64, 128), BF...]
where the time goes in v3:
time: 128 us
  Pallas kernels  128 us (100%)
    pallas_call x1, Pallas kernels, per_device(): pl.pallas_call(kernel, out_shape=jax.ShapeDtypeStruct((2, 6, 64, 128), BF...  126 us

profile of v3, /device:TPU:1, one launch (start us, length us, event | category | flops | bytes accessed | tf_op | source)
XLA Modules:
  0.0 128.2 jit_solution(2448207229409967831)
XLA Ops:
  0.6 125.6 %shard_map.122.ob = bf16[2,6,64,128]{3,2,1,0:T(8,128)(2,1)} custom-call(s32[10]{0:T(128)} %mask.1, bf16[257,4,104]{2,1,0:T(4,128)(2,1)} %bitcast.7, bf16[2,10,104,512]{3,2,1,0:T(8,128)(2,1)} %up_hbm.1, bf16[2,10,104,512]{3,2,1,0:T(8,128)(2,1)} %bitcast.6, f32[10,2,512]{2,1,0:T(2,128)} %bitcast.11, f32[10,2,1664]{2,1,0:T(2,128)} %bitcast.9, ...), custom_call_target="tpu_custom_call" | custom-call | tf_op jit(solution)/shard_map/pallas_call | solution.py:713
  126.3 1.9 %shard_map.123 = (f32[4,22528]{1,0:T(4,128)}, f32[4]{0:T(128)}) custom-call(s32[4]{0:T(128)} %labels.1, bf16[2,6,64,128]{3,2,1,0:T(8,128)(2,1)} %shard_map.122.ob), custom_call_target="tpu_custom_call" | custom-call | tf_op jit(solution)/shard_map/pallas_call | solution.py:775

commit v4 on v3

--- a/solution.py
+++ b/solution.py
@@ -22,6 +22,7 @@
 OWN = 80
 CHUNK = 208
 CLS_BLOCKS = 11
+WORKERS = 6
 UP1, DOWN1, UP2, DOWN2 = 0, 1, 2, 3
 PLACES = ((-1, 0), (1, 0), (0, 1), (-1, 1), (1, 1), (2, 0), (2, 1), (0, 0))
 FAR = (0, -1, 1, -2, 2, -3, 3, 4)
@@ -42,9 +43,9 @@
     mask, tok_hbm, up_hbm, down_hbm, up_b_hbm, down_b_hbm, norm_hbm, final_hbm, proj_hbm, cet_hbm,
     ob_out,
     up_ck, down_ck, tok, up_b, down_b, norm_g, final_gain, cet, a2a, state, x1, x2, gath, w_up1, w_dn1, w_up2, w_dn2, hid, p_sib, s_sib, t_own,
-    red, extra_r, part, part_r, pair, proj, unit_m, unit_r, cls, lg, lr, ob,
+    red, extra_r, pair, proj, unit_m, cls, lg, lr, ob,
     s_a2a, r_a2a, s_ag, r_ag, s_sb, r_sb, s_ring, r_ring, s_far, r_far, s_rs, r_rs, s_half, r_half, s_ex, r_ex,
-    s_pr, r_pr, s_cl, r_cl, s_un, r_un, s_lg, r_lg, s_ob, r_ob,
+    s_pr, r_pr, s_cl, r_cl, s_un, r_un, s_lg, r_lg, s_ob, r_ob, s_os, r_os,
     ck_sem,
 ):
     dp = lax.axis_index("dp")
@@ -105,7 +106,12 @@
         load.start()
 
     state[64:80, :] = jnp.zeros((16, D), F32)
-    ob[1, 5] = jnp.zeros((64, 128), BF16)
+    worker = jnp.logical_and(core == 0, chip < WORKERS)
+
+    @pl.when(chip == WORKERS - 1)
+    def _():
+        cls[1] = jnp.zeros((16, EMBB, 128), BF16)
+
     barrier = pltpu.get_barrier_semaphore()
 
     def greet(k):
@@ -192,6 +198,8 @@
         if step == 0:
             ring_push(t, dp, 0, z_next)
             ring_push(t, dp, 7, z_prev)
+        elif step == 9:
+            far_across(t, 0)
         elif step < 4:
             sl, sr = slot(yh, -step), slot(yh, step)
             ring_got(t, sl, step - 1)
@@ -199,8 +207,6 @@
             ring_got(t, sr, 7 + step - 1)
             if step < 3:
                 ring_push(t, sr, 7 + step, z_prev)
-            if step == 1:
-                far_across(t, 0)
             far_across(t, 2 * step - 1)
             far_across(t, 2 * step)
         elif step == 4:
@@ -366,32 +372,33 @@
     ag_start(0, x1, 1)
     ag_start_extra(0, x1)
     ring(UP1, 1)
+    far_ring(DOWN1, 9)
     ring(UP1, 2)
     own_shard(UP2, up_ck, 1)
-    far_ring(DOWN1, 1)
+    own_shard(DOWN2, down_ck, 1)
     ring(UP1, 3)
     for idx in range(3):
         ag_recv(0, x1, idx, 0)
     ring(UP1, 4)
+    far_ring(DOWN1, 1)
     for idx in range(3):
         ag_recv(0, x1, idx, 1)
-    far_ring(DOWN1, 2)
     ring(UP1, 5)
     ag_recv(0, x1, 3, 0)
     ag_recv(0, x1, 4, 0)
+    far_ring(DOWN1, 2)
     ring(UP1, 6)
-    far_ring(DOWN1, 3)
+    ag_recv(0, x1, 5, 0)
     ag_recv(0, x1, 3, 1)
     ag_recv(0, x1, 4, 1)
-    ag_recv(0, x1, 5, 0)
     ring(UP1, 7)
+    far_ring(DOWN1, 3)
     ag_recv(0, x1, 5, 1)
     ag_recv(0, x1, 6, 0)
-    far_ring(DOWN1, 4)
     ag_recv(0, x1, 6, 1)
     ag_extra(0, x1)
-    own_shard(DOWN2, down_ck, 1)
     ring(UP1, 8)
+    far_ring(DOWN1, 4)
     ring(UP2, 0)
     compact(UP1, w_up1)
     up_b_load.wait()
@@ -399,20 +406,19 @@
     ag_finish(0, x1)
     for ch in range(5):
         hid[CHUNK * ch : CHUNK * ch + CHUNK, :] = up_chunk(x1, w_up1, bias_up1, ch)
-        if ch == 1:
-            ring(UP2, 9)
-        if ch == 3:
-            ring(UP2, 2)
 
     def send_cls(k):
-        @pl.when(k != mp)
-        def _():
-            src = cet.at[:, pl.ds(pl.multiple_of(128 * k, 128), 128)]
-            copy(src, cls.at[mp], s_cl.at[k], r_cl.at[mp], dp, k).start()
-
-        @pl.when(k == mp)
-        def _():
-            cls[mp] = cet[:, pl.ds(pl.multiple_of(128 * k, 128), 128)]
+        to = lax.div(k, 2) * 2
+        src = cet.at[:, pl.ds(pl.multiple_of(128 * k, 128), 128)]
+        n = lax.rem(k, 2)
+
+        @pl.when(to != mp)
+        def _():
+            copy(src, cls.at[n, mp], s_cl.at[k], r_cl.at[n, mp], dp, to).start()
+
+        @pl.when(to == mp)
+        def _():
+            cls[n, mp] = cet[:, pl.ds(pl.multiple_of(128 * k, 128), 128)]
 
     cet_load.wait()
     loop(0, CLS_BLOCKS, send_cls)
@@ -421,8 +427,9 @@
     bias_down1 = soup_vec(down_b, 0, D)
     bias_up2 = soup_vec(up_b, 1, FFB)
     bias_down2 = soup_vec(down_b, 1, D)
+    ring(UP2, 9)
     far_ring(DOWN1, 5)
-    ring(UP2, 1)
+    ring(UP2, 2)
     compact(DOWN1, w_dn1)
 
     def chunk_product(o, c):
@@ -435,8 +442,10 @@
         return pl.ds(0, 144 if STEPS[o] == 0 else 128)
 
     def sib_chunk(o):
+        p_sib[o, chunk_rows(o), :] = chunk_product(o, 1 - core).astype(BF16)
+
+    def sib_send(o):
         rows = chunk_rows(o)
-        p_sib[o, rows, :] = chunk_product(o, 1 - core).astype(BF16)
         copy(p_sib.at[o, rows], s_sib.at[o, rows], s_half.at[o], r_half.at[o], dp, sibling).start()
 
     def own_chunk(o):
@@ -455,29 +464,36 @@
         ag_start(1, x2, h)
 
     sib_chunk(0)
+    sib_send(0)
     sib_chunk(1)
+    ring(UP2, 1)
     own_chunk(0)
     for h in range(2):
         rs_push(0, yl, 0, h, left)
         rs_push(0, 1 - yl, 1, h, right)
-    ring(UP2, 3)
+    sib_send(1)
     sib_chunk(2)
+    sib_send(2)
     own_chunk(1)
     rs_push(1, 1 - yl, 2, 0, left)
     rs_push(1, 1 - yl, 2, 1, left)
     ring(UP2, 4)
+    ring(UP2, 3)
     sib_chunk(3)
+    sib_send(3)
     own_chunk(2)
     for h in range(2):
         rs_add(2, 1 - yl, h, 1)
         rs_push(2, 1 - yl, 3, h, right)
-    ring(UP2, 5)
     for h in range(2):
         rs_add(1, yl, h, 0)
         rs_push(1, yl, 4, h, left)
         rs_push(2, yl, 5, h, right)
     ring(UP2, 6)
     own_chunk(3)
+    ring(UP2, 5)
+    ring(DOWN2, 9)
+    ring(DOWN2, 0)
 
     @pl.when(extra_src)
     def _():
@@ -487,12 +503,9 @@
 
     rs_add(3, 1 - yl, 0, 3, 2)
     rs_push(3, 1 - yl, 6, 0, across)
-    ring(UP2, 7)
-    ring(DOWN2, 0)
     rs_add(3, 1 - yl, 1, 3, 2)
     rs_push(3, 1 - yl, 6, 1, across)
-    ring(UP2, 8)
-    ring(DOWN2, 9)
+    ring(UP2, 7)
     finish_half(0)
     ring(DOWN2, 2)
     finish_half(1)
@@ -515,38 +528,61 @@
     state_sum = jnp.dot(
         jnp.where(inside, 1.0, 0.0).astype(BF16), state[...].astype(BF16), preferred_element_type=F32
     )[:8]
+    hsum = jnp.zeros((16, FFB), F32)
+
+    def pair_sum(c, dx, idxs, with_extra=False):
+        if c is not core:
+            for idx in idxs:
+                for h in range(2):
+                    got(half_rows(x2, 1 - core, idx, h), r_sb.at[1, 2 * idx + h])
+        x = x2[pl.ds(block_rows(c, dx, 0), 128), :]
+        size = 128
+        if with_extra:
+            x = jnp.concatenate([x, x2[1024:1040, :]], axis=0)
+            size = 144
+        h = gelu(jnp.dot(x, w_up2[...], preferred_element_type=F32) + bias_up2).astype(BF16)
+        row = lax.broadcasted_iota(jnp.int32, (16, size), 1)
+        img = lax.broadcasted_iota(jnp.int32, (16, size), 0)
+        inside = ((row & 3) == img) & (row < 132)
+        return jnp.dot(jnp.where(inside, 1.0, 0.0).astype(BF16), h, preferred_element_type=F32)
+
+    other = 1 - core
     ring(DOWN2, 1)
-    ring(DOWN2, 3)
+    ring(UP2, 8)
+    compact(UP2, w_up2)
     for idx in range(3):
         ag_recv(1, x2, idx, 0)
-    compact(UP2, w_up2)
     ring(DOWN2, 4)
     for idx in range(3):
         ag_recv(1, x2, idx, 1)
-    ring(DOWN2, 5)
+    ring(DOWN2, 3)
+    hsum = hsum + pair_sum(core, 0, (7, 2))
+    ring(DOWN2, 6)
     ag_recv(1, x2, 3, 0)
     ag_recv(1, x2, 4, 0)
     ag_recv(1, x2, 5, 0)
-    ring(DOWN2, 6)
+    ring(DOWN2, 5)
     ag_recv(1, x2, 3, 1)
     ag_recv(1, x2, 4, 1)
+    hsum = hsum + pair_sum(core, -1, (0, 3))
+    hsum = hsum + pair_sum(other, 0, (7, 2))
+    ring(DOWN2, 7)
     ag_recv(1, x2, 6, 0)
-    ring(DOWN2, 7)
     ag_recv(1, x2, 5, 1)
+    hsum = hsum + pair_sum(core, 1, (1, 4))
     ag_recv(1, x2, 6, 1)
     ag_extra(1, x2)
-    ag_finish(1, x2)
-    hsum = jnp.zeros((16, FFB), F32)
-    for ch in range(5):
-        h = up_chunk(x2, w_up2, bias_up2, ch)
-        row = lax.broadcasted_iota(jnp.int32, (16, CHUNK), 1) + CHUNK * ch
-        img = lax.broadcasted_iota(jnp.int32, (16, CHUNK), 0)
-        inside = ((row & 3) == img) & (row < 4 * TOKS)
-        hsum = hsum + jnp.dot(
-            jnp.where(inside, 1.0, 0.0).astype(BF16), h, preferred_element_type=F32
-        )
+    hsum = hsum + pair_sum(other, -1, (0, 3))
+    hsum = hsum + pair_sum(core, 2, (5, 6))
     ring(DOWN2, 8)
     compact(DOWN2, w_dn2)
+    hsum = hsum + pair_sum(other, 1, (1, 4))
+
+    @pl.when(core == 0)
+    def _():
+        got(x2.at[pl.ds(1024, 16)], r_sb.at[1, 16])
+
+    hsum = hsum + pair_sum(other, 2, (5, 6), True)
 
     hmean = hsum[:8] * (1.0 / TOKS)
     high = hmean.astype(BF16)
@@ -556,37 +592,41 @@
         (((1,), (1,)), ((), ())), preferred_element_type=F32,
     )
     partial = both[:8] + both[8:] + state_sum * (1.0 / TOKS)
-    part[...] = partial[:4]
-    copy(part, part_r, s_pr.at[0], r_pr.at[0], dp, sibling).start()
-    got(part_r, r_pr.at[0])
-    pair[chip] = (part[...] + part_r[...]).astype(BF16)
-
-    def send_pair(k):
-        copy(
-            pair.at[chip], pair.at[chip], s_pr.at[k], r_pr.at[k], dp, lax.rem(chip + k, 8) * 2 + core
-        ).start()
-
-    loop(1, 8, send_pair)
+    pair[mp] = partial[:4].astype(BF16)
+
+    def send_pair(q):
+        @pl.when(2 * q != mp)
+        def _():
+            copy(pair.at[mp], pair.at[mp], s_pr.at[q], r_pr.at[mp], dp, 2 * q).start()
+
+    loop(0, WORKERS, send_pair)
     final_load.wait()
     proj_load.wait()
-    loop(1, 8, lambda k: got(pair.at[lax.rem(chip + 8 - k, 8)], r_pr.at[k]))
-    pooled = pair[0].astype(F32)
-    for k in range(1, 8):
-        pooled = pooled + pair[k].astype(F32)
-    pooled = (pooled + bias_down2).astype(BF16).astype(F32)
-    pooled = jnp.concatenate([pooled, jnp.zeros_like(pooled)], axis=0)
-    pooled_norm = layer_norm(pooled, final_gain[...].reshape(1, D))
-    pooled_norm = jnp.concatenate([pooled_norm, jnp.zeros_like(pooled_norm)], axis=0).astype(BF16)
-    embedding = jnp.dot(pooled_norm, proj[...], preferred_element_type=F32)[:8]
-    unit = embedding * lax.rsqrt(jnp.sum(embedding * embedding, axis=1, keepdims=True) + 1e-06)
-    first_core = core == 0
-    unit_m[dp] = jnp.where(first_core, unit[:4, :640], unit[:4, 640:]).astype(BF16)
-
-    def send_unit(k):
-        mine = unit_m.at[dp]
-        copy(mine, mine, s_un.at[k], r_un.at[k], lax.rem(dp + k, 16), mp).start()
-
-    loop(1, 16, send_unit)
+
+    @pl.when(worker)
+    def _():
+        def wait_pair(k):
+            @pl.when(k != mp)
+            def _():
+                got(pair.at[k], r_pr.at[k])
+
+        loop(0, 16, wait_pair)
+        pooled = pair[0].astype(F32)
+        for k in range(1, 16):
+            pooled = pooled + pair[k].astype(F32)
+        pooled = (pooled + bias_down2).astype(BF16).astype(F32)
+        pooled = jnp.concatenate([pooled, jnp.zeros_like(pooled)], axis=0)
+        normed = layer_norm(pooled, final_gain[...].reshape(1, D))
+        normed = jnp.concatenate([normed, jnp.zeros_like(normed)], axis=0).astype(BF16)
+        embedding = jnp.dot(normed, proj[...], preferred_element_type=F32)[:8]
+        unit = embedding * lax.rsqrt(jnp.sum(embedding * embedding, axis=1, keepdims=True) + 1e-06)
+        unit_m[dp] = unit[:4].astype(BF16)
+
+        def send_unit(k):
+            mine = unit_m.at[dp]
+            copy(mine, mine, s_un.at[k], r_un.at[k], lax.rem(dp + k, 16), mp).start()
+
+        loop(1, 16, send_unit)
 
     loop(1, 16, lambda k: sent(tok.at[pl.ds(0, 17)], s_a2a.at[k]))
 
@@ -612,36 +652,41 @@
         sent(extra_r.at[0], s_ex.at[0, 0])
 
     def sent_cls(k):
-        @pl.when(k != mp)
-        def _():
-            sent(cls.at[0], s_cl.at[k])
+        @pl.when(lax.div(k, 2) * 2 != mp)
+        def _():
+            sent(cls.at[0, 0], s_cl.at[k])
 
     loop(0, CLS_BLOCKS, sent_cls)
 
-
-    def wait_cls(k):
-        @pl.when(k != mp)
-        def _():
-            got(cls.at[k], r_cl.at[k])
-
-    @pl.when(mp < CLS_BLOCKS)
-    def _():
+    def sent_pair(q):
+        @pl.when(2 * q != mp)
+        def _():
+            sent(pair.at[0], s_pr.at[q])
+
+    loop(0, WORKERS, sent_pair)
+
+    def ob_forward(k):
+        copy(ob.at[k], ob.at[k], s_os.at[k], r_os.at[k], dp, sibling).start()
+
+    @pl.when(worker)
+    def _():
+        def wait_cls(k):
+            @pl.when(k != mp)
+            def _():
+                got(cls.at[0, k], r_cl.at[0, k])
+
+                @pl.when(chip < WORKERS - 1)
+                def _():
+                    got(cls.at[1, k], r_cl.at[1, k])
+
         loop(0, 16, wait_cls)
-
-    loop(1, 16, lambda k: got(unit_m.at[lax.rem(dp + 16 - k, 16)], r_un.at[k]))
-    copy(unit_m, unit_r, s_un.at[0], r_un.at[0], dp, sibling).start()
-    got(unit_r, r_un.at[0])
-
-    @pl.when(mp < CLS_BLOCKS)
-    def _():
-        mine = unit_m[...].astype(F32).reshape(64, 640)
-        rest = unit_r[...].astype(F32).reshape(64, 640)
-        lhs = jnp.concatenate(
-            [jnp.where(first_core, mine, rest), jnp.where(first_core, rest, mine)], axis=1
-        ).astype(BF16)
-        rhs = jnp.concatenate([cls[k] for k in range(16)], axis=0)
+        rhs = jnp.concatenate(
+            [jnp.concatenate([cls[n, k] for k in range(16)], axis=0) for n in range(2)], axis=1
+        )
+        loop(1, 16, lambda k: got(unit_m.at[lax.rem(dp + 16 - k, 16)], r_un.at[k]))
+        lhs = unit_m[...].astype(F32).reshape(64, EMB).astype(BF16)
         scores = jnp.dot(lhs, rhs, preferred_element_type=F32) * 100.0
-        lg[...] = scores.reshape(16, 4, 128)
+        lg[...] = scores.reshape(16, 4, 256)
         lr[dp] = lg[dp]
 
         def send_logits(k):
@@ -654,34 +699,39 @@
             got(lr.at[lax.rem(dp + 16 - k, 16)], r_lg.at[k])
 
         loop(1, 16, wait_logits)
-        ob[core, chip] = lr[...].reshape(64, 128).astype(BF16)
+        ob[chip] = lr[...].reshape(64, 256).astype(BF16)
 
         def send_ob(k):
-            mine = ob.at[core, chip]
-            copy(mine, mine, s_ob.at[k], r_ob.at[chip], dp, lax.rem(chip + k, 8) * 2 + core).start()
+            mine = ob.at[chip]
+            copy(mine, mine, s_ob.at[k], r_ob.at[chip], dp, lax.rem(chip + k, 8) * 2).start()
 
         loop(1, 8, send_ob)
-
-    for k in range(6):
-        @pl.when(jnp.logical_and(chip != k, 2 * k + core < CLS_BLOCKS))
-        def _(k=k):
-            got(ob.at[core, k], r_ob.at[k])
-
-    copy(ob.at[core], ob.at[core], s_ob.at[0], r_ob.at[8], dp, sibling).start()
-    got(ob.at[1 - core], r_ob.at[8])
+        ob_forward(chip)
+
+    @pl.when(core == 0)
+    def _():
+        for k in range(WORKERS):
+            @pl.when(chip != k)
+            def _(k=k):
+                got(ob.at[k], r_ob.at[k])
+                ob_forward(k)
+
+    @pl.when(core == 1)
+    def _():
+        for k in range(WORKERS):
+            got(ob.at[k], r_os.at[k])
+
     ob_out[...] = ob[...]
 
-    loop(1, 16, lambda k: sent(unit_m.at[0], s_un.at[k]))
-    sent(unit_m, s_un.at[0])
-    sent(part, s_pr.at[0])
-    loop(1, 8, lambda k: sent(pair.at[0], s_pr.at[k]))
-
-    @pl.when(mp < CLS_BLOCKS)
-    def _():
+    @pl.when(worker)
+    def _():
+        loop(1, 16, lambda k: sent(unit_m.at[0], s_un.at[k]))
         loop(1, 16, lambda k: sent(lg.at[0], s_lg.at[k]))
-        loop(1, 8, lambda k: sent(ob.at[0, 0], s_ob.at[k]))
-
-    sent(ob.at[0], s_ob.at[0])
+        loop(1, 8, lambda k: sent(ob.at[0], s_ob.at[k]))
+
+    @pl.when(core == 0)
+    def _():
+        loop(0, WORKERS, lambda k: sent(ob.at[0], s_os.at[k]))
 
 
 def finish(labels, ob, out, lab_out):
@@ -692,7 +742,7 @@
     for i in range(1, 4):
         label = jnp.where(row == i, labels[i], label)
     for k in range(CLS_BLOCKS):
-        vals = ob[k % 2, k // 2].astype(F32)
+        vals = ob[k // 2, :, 128 * (k % 2) : 128 * (k % 2) + 128].astype(F32)
         for g in range(16):
             first = (g * CLS_BLOCKS + k) * 128
             piece = vals[4 * g : 4 * g + 4]
@@ -712,7 +762,7 @@
     dma = pltpu.SemaphoreType.DMA
     scores = pl.pallas_call(
         kernel,
-        out_shape=jax.ShapeDtypeStruct((2, 6, 64, 128), BF16),
+        out_shape=jax.ShapeDtypeStruct((WORKERS, 64, 256), BF16),
         in_specs=[sm] + [hbm] * 9,
         out_specs=vm,
         scratch_shapes=[
@@ -739,16 +789,13 @@
             pltpu.VMEM((4, 144, D), BF16),
             pltpu.VMEM((7, 2, 32, D), BF16),
             pltpu.VMEM((8, 16, D), BF16),
-            pltpu.VMEM((4, D), F32),
-            pltpu.VMEM((4, D), F32),
-            pltpu.VMEM((8, 4, D), BF16),
+            pltpu.VMEM((16, 4, D), BF16),
             pltpu.VMEM((D, EMB), BF16),
-            pltpu.VMEM((16, 4, EMB // 2), BF16),
-            pltpu.VMEM((16, 4, EMB // 2), BF16),
-            pltpu.VMEM((16, EMBB, 128), BF16),
-            pltpu.VMEM((16, 4, 128), F32),
-            pltpu.VMEM((16, 4, 128), F32),
-            pltpu.VMEM((2, 6, 64, 128), BF16),
+            pltpu.VMEM((16, 4, EMB), BF16),
+            pltpu.VMEM((2, 16, EMBB, 128), BF16),
+            pltpu.VMEM((16, 4, 256), F32),
+            pltpu.VMEM((16, 4, 256), F32),
+            pltpu.VMEM((WORKERS, 64, 256), BF16),
             dma((16,)), dma((16,)),
             dma((2, 14)), dma((2, 14)),
             dma((2, 17)), dma((2, 17)),
@@ -757,11 +804,12 @@
             dma((14,)), dma((14,)),
             dma((4,)), dma((4,)),
             dma((2, 8)), dma((10,)),
-            dma((8,)), dma((8,)),
+            dma((8,)), dma((16,)),
+            dma((16,)), dma((2, 16)),
             dma((16,)), dma((16,)),
             dma((16,)), dma((16,)),
-            dma((16,)), dma((16,)),
-            dma((8,)), dma((9,)),
+            dma((8,)), dma((8,)),
+            dma((8,)), dma((8,)),
             dma((11,)),
         ],
         compiler_params=pltpu.CompilerParams(

time: 128 us -> 127 us (level)
  Pallas kernels: 128 us -> 126 us
    pallas_call x1, Pallas kernels: 126 us -> 124 us  [per_device(): pl.pallas_call(kernel, out_shape=jax.ShapeDtypeStruct((WORKERS, 64, 256),...]
where the time goes in v4:
time: 127 us; the launch traced here: 126 us
  Pallas kernels  126 us (99%)
    pallas_call x1, Pallas kernels, per_device(): pl.pallas_call(kernel, out_shape=jax.ShapeDtypeStruct((WORKERS, 64, 256),...  124 us

profile of v4, /device:TPU:1, one launch (start us, length us, event | category | flops | bytes accessed | tf_op | source)
XLA Modules:
  0.0 126.5 jit_solution(1240986912791718064)
XLA Ops:
  0.6 123.9 %shard_map.122.ob = bf16[6,64,256]{2,1,0:T(8,128)(2,1)} custom-call(s32[10]{0:T(128)} %mask.1, bf16[257,4,104]{2,1,0:T(4,128)(2,1)} %bitcast.7, bf16[2,10,104,512]{3,2,1,0:T(8,128)(2,1)} %up_hbm.1, bf16[2,10,104,512]{3,2,1,0:T(8,128)(2,1)} %bitcast.6, f32[10,2,512]{2,1,0:T(2,128)} %bitcast.11, f32[10,2,1664]{2,1,0:T(2,128)} %bitcast.9, ...), custom_call_target="tpu_custom_call" | custom-call | tf_op jit(solution)/shard_map/pallas_call | solution.py:763
  124.6 1.9 %shard_map.123 = (f32[4,22528]{1,0:T(4,128)}, f32[4]{0:T(128)}) custom-call(s32[4]{0:T(128)} %labels.1, bf16[6,64,256]{2,1,0:T(8,128)(2,1)} %shard_map.122.ob), custom_call_target="tpu_custom_call" | custom-call | tf_op jit(solution)/shard_map/pallas_call | solution.py:823

commit v5 on v4

--- a/solution.py
+++ b/solution.py
@@ -203,14 +203,22 @@
         elif step < 4:
             sl, sr = slot(yh, -step), slot(yh, step)
             ring_got(t, sl, step - 1)
-            ring_push(t, sl, step, z_next)
+            if step < 3:
+                ring_push(t, sl, step, z_next)
+            else:
+                rows = gath.at[t, sl, pl.ds(0, 112)]
+                copy(rows, rows, s_ring.at[t, 3], r_ring.at[t, 3], z_next, mp).start()
             ring_got(t, sr, 7 + step - 1)
             if step < 3:
                 ring_push(t, sr, 7 + step, z_prev)
+            else:
+                rows = gath.at[t, sr, pl.ds(112, 96)]
+                copy(rows, rows, s_ring.at[t, 10], r_ring.at[t, 10], z_prev, mp).start()
             far_across(t, 2 * step - 1)
             far_across(t, 2 * step)
         elif step == 4:
-            ring_got(t, slot(yh, 4), 3)
+            got(gath.at[t, slot(yh, 4), pl.ds(0, 112)], r_ring.at[t, 3])
+            got(gath.at[t, slot(yh, 4), pl.ds(112, 96)], r_ring.at[t, 10])
             far_across(t, 7)
         else:
             for k in range(8):
@@ -376,30 +384,31 @@
     ring(UP1, 2)
     own_shard(UP2, up_ck, 1)
     own_shard(DOWN2, down_ck, 1)
+    far_ring(DOWN1, 1)
     ring(UP1, 3)
     for idx in range(3):
         ag_recv(0, x1, idx, 0)
+    far_ring(DOWN1, 2)
     ring(UP1, 4)
-    far_ring(DOWN1, 1)
     for idx in range(3):
         ag_recv(0, x1, idx, 1)
     ring(UP1, 5)
     ag_recv(0, x1, 3, 0)
     ag_recv(0, x1, 4, 0)
-    far_ring(DOWN1, 2)
-    ring(UP1, 6)
+    far_ring(DOWN1, 3)
     ag_recv(0, x1, 5, 0)
     ag_recv(0, x1, 3, 1)
     ag_recv(0, x1, 4, 1)
-    ring(UP1, 7)
-    far_ring(DOWN1, 3)
+    ring(UP1, 6)
+    far_ring(DOWN1, 4)
     ag_recv(0, x1, 5, 1)
     ag_recv(0, x1, 6, 0)
     ag_recv(0, x1, 6, 1)
     ag_extra(0, x1)
+    ring(UP1, 7)
+    ring(UP2, 0)
     ring(UP1, 8)
-    far_ring(DOWN1, 4)
-    ring(UP2, 0)
+    ring(UP2, 9)
     compact(UP1, w_up1)
     up_b_load.wait()
     bias_up1 = soup_vec(up_b, 0, FFB)
@@ -427,7 +436,6 @@
     bias_down1 = soup_vec(down_b, 0, D)
     bias_up2 = soup_vec(up_b, 1, FFB)
     bias_down2 = soup_vec(down_b, 1, D)
-    ring(UP2, 9)
     far_ring(DOWN1, 5)
     ring(UP2, 2)
     compact(DOWN1, w_dn1)
@@ -466,7 +474,6 @@
     sib_chunk(0)
     sib_send(0)
     sib_chunk(1)
-    ring(UP2, 1)
     own_chunk(0)
     for h in range(2):
         rs_push(0, yl, 0, h, left)
@@ -474,11 +481,13 @@
     sib_send(1)
     sib_chunk(2)
     sib_send(2)
+    ring(UP2, 1)
     own_chunk(1)
     rs_push(1, 1 - yl, 2, 0, left)
     rs_push(1, 1 - yl, 2, 1, left)
     ring(UP2, 4)
-    ring(UP2, 3)
+    ring(DOWN2, 9)
+    ring(DOWN2, 0)
     sib_chunk(3)
     sib_send(3)
     own_chunk(2)
@@ -489,11 +498,9 @@
         rs_add(1, yl, h, 0)
         rs_push(1, yl, 4, h, left)
         rs_push(2, yl, 5, h, right)
+    ring(UP2, 3)
+    own_chunk(3)
     ring(UP2, 6)
-    own_chunk(3)
-    ring(UP2, 5)
-    ring(DOWN2, 9)
-    ring(DOWN2, 0)
 
     @pl.when(extra_src)
     def _():
@@ -503,12 +510,15 @@
 
     rs_add(3, 1 - yl, 0, 3, 2)
     rs_push(3, 1 - yl, 6, 0, across)
+    ring(DOWN2, 2)
     rs_add(3, 1 - yl, 1, 3, 2)
     rs_push(3, 1 - yl, 6, 1, across)
+    ring(UP2, 5)
+    ring(DOWN2, 1)
+    finish_half(0)
+    ring(DOWN2, 4)
+    finish_half(1)
     ring(UP2, 7)
-    finish_half(0)
-    ring(DOWN2, 2)
-    finish_half(1)
 
     @pl.when(last)
     def _():
@@ -547,26 +557,24 @@
         return jnp.dot(jnp.where(inside, 1.0, 0.0).astype(BF16), h, preferred_element_type=F32)
 
     other = 1 - core
-    ring(DOWN2, 1)
+    for idx in range(3):
+        ag_recv(1, x2, idx, 0)
+    ring(DOWN2, 3)
+    for idx in range(3):
+        ag_recv(1, x2, idx, 1)
     ring(UP2, 8)
     compact(UP2, w_up2)
-    for idx in range(3):
-        ag_recv(1, x2, idx, 0)
-    ring(DOWN2, 4)
-    for idx in range(3):
-        ag_recv(1, x2, idx, 1)
-    ring(DOWN2, 3)
-    hsum = hsum + pair_sum(core, 0, (7, 2))
     ring(DOWN2, 6)
     ag_recv(1, x2, 3, 0)
     ag_recv(1, x2, 4, 0)
     ag_recv(1, x2, 5, 0)
+    hsum = hsum + pair_sum(core, 0, (7, 2))
     ring(DOWN2, 5)
     ag_recv(1, x2, 3, 1)
     ag_recv(1, x2, 4, 1)
+    ring(DOWN2, 7)
     hsum = hsum + pair_sum(core, -1, (0, 3))
     hsum = hsum + pair_sum(other, 0, (7, 2))
-    ring(DOWN2, 7)
     ag_recv(1, x2, 6, 0)
     ag_recv(1, x2, 5, 1)
     hsum = hsum + pair_sum(core, 1, (1, 4))
@@ -638,7 +646,9 @@
 
     for t in (UP1, UP2, DOWN2):
         sent_ring(t)
-    loop(0, 4, lambda n: sent(gath.at[0, 0], s_ring.at[DOWN1, n]))
+    loop(0, 3, lambda n: sent(gath.at[0, 0], s_ring.at[DOWN1, n]))
+    sent(gath.at[0, 0, pl.ds(0, 112)], s_ring.at[DOWN1, 3])
+    sent(gath.at[0, 0, pl.ds(0, 96)], s_ring.at[DOWN1, 10])
     loop(7, 10, lambda n: sent(gath.at[0, 0], s_ring.at[DOWN1, n]))
     loop(0, 8, lambda n: sent(gath.at[0, 0], s_far.at[n]))
     ag_sent(0, x1)

time: 127 us -> 120 us (0.945)
  Pallas kernels: 126 us -> 120 us
    pallas_call x1, Pallas kernels: 124 us -> 118 us  [per_device(): pl.pallas_call(kernel, out_shape=jax.ShapeDtypeStruct((WORKERS, 64, 256),...]
where the time goes in v5:
time: 120 us
  Pallas kernels  120 us (100%)
    pallas_call x1, Pallas kernels, per_device(): pl.pallas_call(kernel, out_shape=jax.ShapeDtypeStruct((WORKERS, 64, 256),...  118 us

profile of v5, /device:TPU:1, one launch (start us, length us, event | category | flops | bytes accessed | tf_op | source)
XLA Modules:
  0.0 120.3 jit_solution(9849974312887927270)
XLA Ops:
  0.6 117.8 %shard_map.122.ob = bf16[6,64,256]{2,1,0:T(8,128)(2,1)} custom-call(s32[10]{0:T(128)} %mask.1, bf16[257,4,104]{2,1,0:T(4,128)(2,1)} %bitcast.7, bf16[2,10,104,512]{3,2,1,0:T(8,128)(2,1)} %up_hbm.1, bf16[2,10,104,512]{3,2,1,0:T(8,128)(2,1)} %bitcast.6, f32[10,2,512]{2,1,0:T(2,128)} %bitcast.11, f32[10,2,1664]{2,1,0:T(2,128)} %bitcast.9, ...), custom_call_target="tpu_custom_call" | custom-call | tf_op jit(solution)/shard_map/pallas_call | solution.py:773
  118.4 1.9 %shard_map.123 = (f32[4,22528]{1,0:T(4,128)}, f32[4]{0:T(128)}) custom-call(s32[4]{0:T(128)} %labels.1, bf16[6,64,256]{2,1,0:T(8,128)(2,1)} %shard_map.122.ob), custom_call_target="tpu_custom_call" | custom-call | tf_op jit(solution)/shard_map/pallas_call | solution.py:833

commit v6 on v5

--- a/solution.py
+++ b/solution.py
@@ -84,6 +84,18 @@
 
         lax.fori_loop(lo, hi, step, 0)
 
+    barrier = pltpu.get_barrier_semaphore()
+
+    def greet(k):
+        pl.semaphore_signal(
+            barrier, inc=1, device_id={"dp": dp, "mp": lax.rem(mp + k, 16)}, device_id_type=MESH
+        )
+        pl.semaphore_signal(
+            barrier, inc=1, device_id={"dp": lax.rem(dp + k, 16), "mp": mp}, device_id_type=MESH
+        )
+
+    loop(1, 16, greet)
+
     loads = [
         pltpu.make_async_copy(src.at[layer], dst.at[layer], ck_sem.at[n])
         for n, (src, dst, layer) in enumerate(
@@ -99,8 +111,9 @@
             )
         )
     )
+    loads[0].start()
     tok_load.start()
-    for load in loads:
+    for load in loads[1:]:
         load.start()
     for load in (norm_load, up_b_load, cet_load, down_b_load, final_load, proj_load):
         load.start()
@@ -111,18 +124,6 @@
     @pl.when(chip == WORKERS - 1)
     def _():
         cls[1] = jnp.zeros((16, EMBB, 128), BF16)
-
-    barrier = pltpu.get_barrier_semaphore()
-
-    def greet(k):
-        pl.semaphore_signal(
-            barrier, inc=1, device_id={"dp": dp, "mp": lax.rem(mp + k, 16)}, device_id_type=MESH
-        )
-        pl.semaphore_signal(
-            barrier, inc=1, device_id={"dp": lax.rem(dp + k, 16), "mp": mp}, device_id_type=MESH
-        )
-
-    loop(1, 16, greet)
 
     mask_f = [mask[i].astype(F32) for i in range(CKPT)]
     total = mask_f[0]
@@ -154,11 +155,15 @@
     def slot(which_yh, shift):
         return which_yh * 8 + lax.rem(z + shift + 8, 8)
 
+    def ring_rows(t, s):
+        return gath.at[t, s, pl.ds(0, 144)] if t == DOWN2 else gath.at[t, s]
+
     def ring_push(t, s, n, to):
-        copy(gath.at[t, s], gath.at[t, s], s_ring.at[t, n], r_ring.at[t, n], to, mp).start()
+        rows = ring_rows(t, s)
+        copy(rows, rows, s_ring.at[t, n], r_ring.at[t, n], to, mp).start()
 
     def ring_got(t, s, n):
-        got(gath.at[t, s], r_ring.at[t, n])
+        got(ring_rows(t, s), r_ring.at[t, n])
 
     def ring(t, step):
         if step == 9:
@@ -188,41 +193,58 @@
             ring_got(t, slot(yh, 4), 6)
             ring_got(t, slot(other_yh, 4), 13)
 
+    def far_part(t):
+        return (0, 208, 112) if t == DOWN1 else (144, 64, 32)
+
+    def far_rows(t, s):
+        first, size, _ = far_part(t)
+        return gath.at[t, s, pl.ds(first, size)]
+
+    def far_halves(t, s):
+        first, size, half = far_part(t)
+        return gath.at[t, s, pl.ds(first, half)], gath.at[t, s, pl.ds(first + half, size - half)]
+
     def far_across(t, k):
-        s = slot(yh, FAR[k])
-        copy(
-            gath.at[t, s], gath.at[t, s], s_far.at[k], r_far.at[k], other_yh * 8 + z, mp
-        ).start()
+        rows = far_rows(t, slot(yh, FAR[k]))
+        copy(rows, rows, s_far.at[t // 2, k], r_far.at[t // 2, k], other_yh * 8 + z, mp).start()
 
     def far_ring(t, step):
+        f = 4 + t // 2
+
+        def push(rows, n, to):
+            copy(rows, rows, s_ring.at[f, n], r_ring.at[f, n], to, mp).start()
+
         if step == 0:
-            ring_push(t, dp, 0, z_next)
-            ring_push(t, dp, 7, z_prev)
+            push(far_rows(t, dp), 0, z_next)
+            push(far_rows(t, dp), 7, z_prev)
         elif step == 9:
             far_across(t, 0)
         elif step < 4:
             sl, sr = slot(yh, -step), slot(yh, step)
-            ring_got(t, sl, step - 1)
-            if step < 3:
-                ring_push(t, sl, step, z_next)
-            else:
-                rows = gath.at[t, sl, pl.ds(0, 112)]
-                copy(rows, rows, s_ring.at[t, 3], r_ring.at[t, 3], z_next, mp).start()
-            ring_got(t, sr, 7 + step - 1)
-            if step < 3:
-                ring_push(t, sr, 7 + step, z_prev)
-            else:
-                rows = gath.at[t, sr, pl.ds(112, 96)]
-                copy(rows, rows, s_ring.at[t, 10], r_ring.at[t, 10], z_prev, mp).start()
+            got(far_rows(t, sl), r_ring.at[f, step - 1])
+            push(far_rows(t, sl) if step < 3 else far_halves(t, sl)[0], step, z_next)
+            got(far_rows(t, sr), r_ring.at[f, 7 + step - 1])
+            push(far_rows(t, sr) if step < 3 else far_halves(t, sr)[1], 7 + step, z_prev)
             far_across(t, 2 * step - 1)
             far_across(t, 2 * step)
         elif step == 4:
-            got(gath.at[t, slot(yh, 4), pl.ds(0, 112)], r_ring.at[t, 3])
-            got(gath.at[t, slot(yh, 4), pl.ds(112, 96)], r_ring.at[t, 10])
+            first, second = far_halves(t, slot(yh, 4))
+            got(first, r_ring.at[f, 3])
+            got(second, r_ring.at[f, 10])
             far_across(t, 7)
         else:
             for k in range(8):
-                got(gath.at[t, slot(other_yh, FAR[k])], r_far.at[k])
+                got(far_rows(t, slot(other_yh, FAR[k])), r_far.at[t // 2, k])
+
+    def far_sent(t):
+        f = 4 + t // 2
+        rows = far_rows(t, 0)
+        loop(0, 3, lambda n: sent(rows, s_ring.at[f, n]))
+        loop(7, 10, lambda n: sent(rows, s_ring.at[f, n]))
+        first, second = far_halves(t, 0)
+        sent(first, s_ring.at[f, 3])
+        sent(second, s_ring.at[f, 10])
+        loop(0, 8, lambda n: sent(rows, s_far.at[t // 2, n]))
 
     def compact(t, dst):
         def pair(j):
@@ -479,6 +501,8 @@
         rs_push(0, yl, 0, h, left)
         rs_push(0, 1 - yl, 1, h, right)
     sib_send(1)
+    far_ring(DOWN2, 0)
+    far_ring(DOWN2, 9)
     sib_chunk(2)
     sib_send(2)
     ring(UP2, 1)
@@ -499,6 +523,7 @@
         rs_push(1, yl, 4, h, left)
         rs_push(2, yl, 5, h, right)
     ring(UP2, 3)
+    far_ring(DOWN2, 1)
     own_chunk(3)
     ring(UP2, 6)
 
@@ -515,9 +540,10 @@
     rs_push(3, 1 - yl, 6, 1, across)
     ring(UP2, 5)
     ring(DOWN2, 1)
+    far_ring(DOWN2, 2)
     finish_half(0)
+    finish_half(1)
     ring(DOWN2, 4)
-    finish_half(1)
     ring(UP2, 7)
 
     @pl.when(last)
@@ -562,16 +588,18 @@
     ring(DOWN2, 3)
     for idx in range(3):
         ag_recv(1, x2, idx, 1)
+    far_ring(DOWN2, 3)
     ring(UP2, 8)
     compact(UP2, w_up2)
     ring(DOWN2, 6)
+    ring(DOWN2, 5)
     ag_recv(1, x2, 3, 0)
     ag_recv(1, x2, 4, 0)
     ag_recv(1, x2, 5, 0)
     hsum = hsum + pair_sum(core, 0, (7, 2))
-    ring(DOWN2, 5)
     ag_recv(1, x2, 3, 1)
     ag_recv(1, x2, 4, 1)
+    far_ring(DOWN2, 4)
     ring(DOWN2, 7)
     hsum = hsum + pair_sum(core, -1, (0, 3))
     hsum = hsum + pair_sum(other, 0, (7, 2))
@@ -583,6 +611,7 @@
     hsum = hsum + pair_sum(other, -1, (0, 3))
     hsum = hsum + pair_sum(core, 2, (5, 6))
     ring(DOWN2, 8)
+    far_ring(DOWN2, 5)
     compact(DOWN2, w_dn2)
     hsum = hsum + pair_sum(other, 1, (1, 4))
 
@@ -638,19 +667,10 @@
 
     loop(1, 16, lambda k: sent(tok.at[pl.ds(0, 17)], s_a2a.at[k]))
 
-    def sent_ring(t):
-        def step(n):
-            sent(gath.at[t, 0], s_ring.at[t, n])
-
-        loop(0, 15, step)
-
     for t in (UP1, UP2, DOWN2):
-        sent_ring(t)
-    loop(0, 3, lambda n: sent(gath.at[0, 0], s_ring.at[DOWN1, n]))
-    sent(gath.at[0, 0, pl.ds(0, 112)], s_ring.at[DOWN1, 3])
-    sent(gath.at[0, 0, pl.ds(0, 96)], s_ring.at[DOWN1, 10])
-    loop(7, 10, lambda n: sent(gath.at[0, 0], s_ring.at[DOWN1, n]))
-    loop(0, 8, lambda n: sent(gath.at[0, 0], s_far.at[n]))
+        loop(0, 15, lambda n, t=t: sent(ring_rows(t, 0), s_ring.at[t, n]))
+    far_sent(DOWN1)
+    far_sent(DOWN2)
     ag_sent(0, x1)
     ag_sent(1, x2)
     for o in range(4):
@@ -717,6 +737,8 @@
 
         loop(1, 8, send_ob)
         ob_forward(chip)
+        loop(1, 16, lambda k: sent(unit_m.at[0], s_un.at[k]))
+        loop(1, 16, lambda k: sent(lg.at[0], s_lg.at[k]))
 
     @pl.when(core == 0)
     def _():
@@ -735,8 +757,6 @@
 
     @pl.when(worker)
     def _():
-        loop(1, 16, lambda k: sent(unit_m.at[0], s_un.at[k]))
-        loop(1, 16, lambda k: sent(lg.at[0], s_lg.at[k]))
         loop(1, 8, lambda k: sent(ob.at[0], s_ob.at[k]))
 
     @pl.when(core == 0)
@@ -809,8 +829,8 @@
             dma((16,)), dma((16,)),
             dma((2, 14)), dma((2, 14)),
             dma((2, 17)), dma((2, 17)),
-            dma((4, 15)), dma((4, 15)),
-            dma((8,)), dma((8,)),
+            dma((6, 15)), dma((6, 15)),
+            dma((2, 8)), dma((2, 8)),
             dma((14,)), dma((14,)),
             dma((4,)), dma((4,)),
             dma((2, 8)), dma((10,)),

time: 120 us -> 118 us (0.983)
  Pallas kernels: 120 us -> 118 us
    pallas_call x1, Pallas kernels: 118 us -> 116 us  [per_device(): pl.pallas_call(kernel, out_shape=jax.ShapeDtypeStruct((WORKERS, 64, 256),...]
where the time goes in v6:
time: 118 us
  Pallas kernels  118 us (100%)
    pallas_call x1, Pallas kernels, per_device(): pl.pallas_call(kernel, out_shape=jax.ShapeDtypeStruct((WORKERS, 64, 256),...  116 us

profile of v6, /device:TPU:1, one launch (start us, length us, event | category | flops | bytes accessed | tf_op | source)
XLA Modules:
  0.0 118.4 jit_solution(7518590249579891819)
XLA Ops:
  0.6 115.8 %shard_map.122.ob = bf16[6,64,256]{2,1,0:T(8,128)(2,1)} custom-call(s32[10]{0:T(128)} %mask.1, bf16[257,4,104]{2,1,0:T(4,128)(2,1)} %bitcast.7, bf16[2,10,104,512]{3,2,1,0:T(8,128)(2,1)} %up_hbm.1, bf16[2,10,104,512]{3,2,1,0:T(8,128)(2,1)} %bitcast.6, f32[10,2,512]{2,1,0:T(2,128)} %bitcast.11, f32[10,2,1664]{2,1,0:T(2,128)} %bitcast.9, ...), custom_call_target="tpu_custom_call" | custom-call | tf_op jit(solution)/shard_map/pallas_call | solution.py:793
  116.5 1.9 %shard_map.123 = (f32[4,22528]{1,0:T(4,128)}, f32[4]{0:T(128)}) custom-call(s32[4]{0:T(128)} %labels.1, bf16[6,64,256]{2,1,0:T(8,128)(2,1)} %shard_map.122.ob), custom_call_target="tpu_custom_call" | custom-call | tf_op jit(solution)/shard_map/pallas_call | solution.py:853
